TPU v7x, 32 devices: a whole 2x2x4 slice. The times are simulated.
32 devices in a mesh: groups: 2 (over y), batch: 4 (over z), mp: 4 (over x, core).
Axes of the slice: x: 2, y: 2, z: 4, core: 2. Of those that a mesh axis runs over, the one named last changes fastest.
Arguments:
- codes: bfloat16 [512, 26624], P(('groups', 'batch'), 'mp'), parts along dimension 0, may hold values from -127 to 127, as said below
- token_scale: float32 [512], P(('groups', 'mp')), parts along dimension 0, may hold values from 0.005 to 0.05
- weight_codes: bfloat16 [26624, 8192], P('mp', 'batch'), may hold values from -127 to 127, as said below
- weight_scale: float32 [8192], P('batch'), may hold values from 1.8385888e-05 to 0.00018385888
- smoothing: float32 [26624], P(('mp', 'batch')), may hold values from 0.25 to 4
Outputs:
- projected: bfloat16 [512, 8192], P(('groups', 'mp'), 'batch'), parts along dimension 0
There are 2 independent parts, one for each index of `groups`. A program takes and returns all parts, laid end to end along the dimension named above; an argument that names none is the same for every part. Nothing has to cross between parts.
Inputs may be any that keep to these rules, and one draw needn't show every extreme that they name: `codes`: whole numbers. `weight_codes`: whole numbers.
All inputs are finite; a program needn't handle non-finite values.
Results may differ from a plain program's by a relative error of at most 0.0049.
Values may be sent and summed in bfloat16 or wider, within the bound.
No kernel may reach another device: no remote copies, remote signals or barrier semaphores. Data moves between devices by JAX's collectives and lax.ppermute only.
A program may use at most 128 MiB of HBM per device.

v0:
```python
import jax
import jax.numpy as jnp
from jax import lax
from jax.sharding import PartitionSpec as P


def per_device(codes, token_scale, weight_codes, weight_scale, smoothing):
    factors = lax.all_gather(smoothing, "batch", axis=0, tiled=True)
    partial_value = jnp.dot(
        (
            lax.all_gather(codes, "batch", axis=0, tiled=True).astype(jnp.float32)
            * factors[None, :]
        ).astype(jnp.bfloat16),
        weight_codes,
        preferred_element_type=jnp.float32,
    )
    total = lax.psum_scatter(partial_value, "mp", scatter_dimension=0, tiled=True)
    scaled = total * token_scale[:, None] * weight_scale[None, :]
    return scaled.astype(jnp.bfloat16)


def solution(mesh):
    in_specs = (
        P(("groups", "batch"), "mp"),
        P(("groups", "mp")),
        P("mp", "batch"),
        P("batch"),
        P(("mp", "batch")),
    )
    out_specs = P(("groups", "mp"), "batch")
    return jax.shard_map(
        per_device, mesh=mesh, in_specs=in_specs, out_specs=out_specs, check_vma=False
    )
```

profile of v0, /device:TPU:0, one launch (start us, length us, event | category | flops | bytes accessed | tf_op | source)
XLA Modules:
  0.0 132.8 jit_solution(16197144158511480353)
XLA Ops:
  6.5 0.0 all-gather.3.cloned.1.call-start
  6.5 0.7 all-gather.3.cloned.1.call-update
  7.3 0.0 reduce-scatter.2.cloned.1.call-start
  7.3 0.7 reshape.3
  8.0 14.8 %all-gather = f32[4,1,1664]{2,1,0:T(1,128)S(1)} all-gather(f32[1,1,1664]{2,1,0:T(1,128)S(1)} %reshape.3), channel_id=1, replica_groups=mesh['groups'=2,'batch'=4,'mp'=4] {'batch'}, dimensions={0}, use_global_device_ids=true | all-gather | bytes 33280 | tf_op jit(solution)/shard_map/all_gather | solution.py:8
  22.8 0.1 reduce
  22.9 0.0 copy-start
  22.9 0.0 copy-start.1
  22.9 56.6 %all-gather.3.cloned.1.call-done = bf16[256,6656]{1,0:T(8,128)(2,1)} async-done(((bf16[64,6656]{1,0:T(8,128)(2,1)}), bf16[256,6656]{1,0:T(8,128)(2,1)}) %all-gather.3.cloned.1.call-update) | async-done | bytes 3407888 | tf_op jit(solution)/shard_map/all_gather | solution.py:11
  79.5 14.4 %fusion = f32[256,2048]{1,0:T(8,128)} fusion(bf16[6656,2048]{1,0:T(8,128)(2,1)} %param.7, bf16[256,6656]{1,0:T(8,128)(2,1)} %all-gather.3.cloned.1.call-done, f32[6656]{0:T(1024)S(1)} %reshape.4), kind=kOutput, calls=%fused_computation.1 | convolution fusion | flops 6984433664 | bytes 32794624 | tf_op jit(solution)/shard_map/dot_general | solution.py:9
  93.9 0.0 reduce-scatter.2.cloned.1.call-update
  93.9 30.2 %reduce-scatter.2.cloned.1.call-done = f32[64,2048]{1,0:T(8,128)} async-done(((f32[256,2048]{1,0:T(8,128)}), f32[64,2048]{1,0:T(8,128)}) %reduce-scatter.2.cloned.1.call-update) | async-done | bytes 524304 | tf_op jit(solution)/shard_map/reduce_scatter | solution.py:17
  124.1 0.0 copy-done
  124.1 0.0 copy-done.1
  124.2 1.9 %multiply_convert_fusion.2 = bf16[64,2048]{1,0:T(8,128)(2,1)} fusion(f32[64,2048]{1,0:T(8,128)} %reduce-scatter.2.cloned.1.call-done, f32[2048]{0:T(1024)S(1)} %copy-done, f32[64]{0:T(128)S(1)} %copy-done.1), kind=kLoop, calls=%fused_computation.3 | loop fusion | flops 393216 | bytes 794880 | tf_op jit(solution)/shard_map/convert_element_type | solution.py:19
  (1 shorter events, 0.0 us)
Async XLA Ops:
  6.5 73.0 %all-gather.3.cloned.1.call-start = ((), (), s32[]{:S(2)}) async-start(), calls=%async_computation.1 | async-start | bytes 4259840 | tf_op jit(solution)/shard_map/all_gather | solution.py:11
  7.3 116.9 %reduce-scatter.2.cloned.1.call-start = ((), (), s32[]{:S(2)}) async-start(), calls=%async_computation.2 | async-start | bytes 2621440 | tf_op jit(solution)/shard_map/reduce_scatter | solution.py:17
  22.9 101.2 %copy-start = (f32[2048]{0:T(1024)S(1)}, f32[2048]{0:T(1024)}, u32[]{:S(2)}) copy-start(f32[2048]{0:T(1024)} %param.8) | copy-start | bytes 24580
  22.9 101.2 %copy-start.1 = (f32[64]{0:T(128)S(1)}, f32[64]{0:T(128)}, u32[]{:S(2)}) copy-start(f32[64]{0:T(128)} %param.6) | copy-start | bytes 772
Sparse Core Ops, SparseCore 0:
  8.9 70.5 all-gather.2
  94.1 30.0 reduce-scatter.1
where the time goes:
time: 133 us
  waiting for transfers between devices  87.5 us (66%)
  blocking collectives  14.8 us (11%)
  matrix products  14.4 us (11%)
  between operations  13.4 us (10%)
  other arithmetic  1.93 us (1%)
    all_gather x1, waiting for transfers between devices, per_device(): lax.all_gather(codes, 'batch', axis=0, tiled=True).astype(jnp.float32)  56.6 us
    reduce_scatter x1, waiting for transfers between devices, per_device(): lax.psum_scatter(partial_value, 'mp', scatter_dimension=0, tiled=True)  30.2 us
    all_gather x1, blocking collectives, per_device(): factors = lax.all_gather(smoothing, 'batch', axis=0, tiled=True)  14.8 us
    dot_general x1, matrix products, per_device(): jnp.dot((lax.all_gather(codes, 'batch', axis=0, tiled=True).astype(jnp.fl...  14.4 us
  transfers between devices with their start and end apart: 2, of which 2 were waited for; matrix products, arithmetic and copies ran while one was open for 1% of the time, Pallas kernels for 0%

commit v1 on v0

--- a/solution.py
+++ b/solution.py
@@ -1,10 +1,19 @@
 import jax
 import jax.numpy as jnp
 from jax import lax
+from jax.experimental import pallas as pl
+from jax.experimental.pallas import tpu as pltpu
 from jax.sharding import PartitionSpec as P
 
-
-def per_device(codes, token_scale, weight_codes, weight_scale, smoothing):
+LANES = 128
+VMEM = 44 << 20
+SMALL = 1 << 20
+OUTER = [(0, 1), (1, 0), (2, 3), (3, 2)]
+INNER = [(1, 2), (2, 1)]
+ENDS = [(1, 0), (2, 3)]
+
+
+def general(codes, token_scale, weight_codes, weight_scale, smoothing):
     factors = lax.all_gather(smoothing, "batch", axis=0, tiled=True)
     partial_value = jnp.dot(
         (
@@ -19,7 +28,228 @@
     return scaled.astype(jnp.bfloat16)
 
 
+def pieces_of(cols):
+    sizes, left = [512], cols - 512
+    while left > 1536:
+        sizes.append(1024)
+        left -= 1024
+    while left > 512:
+        sizes.append(512)
+        left -= 512
+    if left > 0:
+        sizes.append(left)
+    out, at = [], 0
+    for size in sizes:
+        out.append((at, size))
+        at += size
+    return out
+
+
+def mm_kernel(place, first, pieces, n_x, n_s, n_after, has_add, n_out, split, *refs):
+    xs, refs = refs[:n_x], refs[n_x:]
+    ss, refs = refs[:n_s], refs[n_s:]
+    w_hbm, refs = refs[0], refs[1 + n_after :]
+    add = None
+    if has_add:
+        add, refs = refs[0], refs[1:]
+    outs, refs = refs[:n_out], refs[n_out:]
+    x_v, s_v, w_v, acc, sem_x, sem_s, sem_w = refs
+    copy_w = [
+        pltpu.make_async_copy(
+            w_hbm.at[pl.ds(first + at, size)], w_v.at[pl.ds(at, size)], sem_w.at[i]
+        )
+        for i, (at, size) in enumerate(pieces)
+    ]
+    n = ss[0].shape[1]
+    z = lax.axis_index("batch")
+    copy_s = [
+        pltpu.make_async_copy(
+            ref,
+            s_v.at[:, pl.ds(pl.multiple_of(lax.rem(z + 4 - k, 4) * n, n), n)],
+            sem_s.at[k],
+        )
+        for k, ref in enumerate(ss)
+    ]
+    copy_w[0].start()
+    for copy in copy_s:
+        copy.start()
+    wait_x = place(xs, x_v, sem_x)
+    for copy in copy_w[1:]:
+        copy.start()
+    for copy in copy_s:
+        copy.wait()
+    wait_x()
+    for i, (at, size) in enumerate(pieces):
+        part = slice(at, at + size)
+        s = s_v[:, first + at : first + at + size]
+        x = (x_v[:, part].astype(jnp.float32) * s).astype(jnp.bfloat16)
+        copy_w[i].wait()
+        y = jnp.dot(x, w_v[part, :], preferred_element_type=jnp.float32)
+        if i == 0:
+            acc[...] = y if add is None else y + add[...]
+        elif i < len(pieces) - 1:
+            acc[...] += y
+        else:
+            y = acc[...] + y
+            at = 0
+            for out, rows in zip(outs, split):
+                out[...] = y[at : at + rows].astype(out.dtype)
+                at += rows
+
+
+def mm(place, xs, ss, w, first, cols, split, out_type, add=None, name="mm"):
+    pieces = pieces_of(cols)
+    width = w.shape[1]
+    rows = sum(split)
+    body = lambda *refs: mm_kernel(
+        place, first, pieces, len(xs), len(ss), 0, add is not None, len(split), split, *refs
+    )
+    anywhere = pl.BlockSpec(memory_space=pl.ANY)
+    vmem = pl.BlockSpec(memory_space=pltpu.VMEM)
+    return pl.pallas_call(
+        body,
+        out_shape=[jax.ShapeDtypeStruct((r, width), out_type) for r in split],
+        in_specs=[anywhere] * (len(xs) + len(ss) + 1) + ([vmem] if add is not None else []),
+        out_specs=[vmem] * len(split),
+        scratch_shapes=[
+            pltpu.VMEM((rows, cols), jnp.bfloat16),
+            pltpu.VMEM((1, sum(s.shape[1] for s in ss)), jnp.float32),
+            pltpu.VMEM((cols, width), jnp.bfloat16),
+            pltpu.VMEM((rows, width), jnp.float32),
+            pltpu.SemaphoreType.DMA((3,)),
+            pltpu.SemaphoreType.DMA((len(ss),)),
+            pltpu.SemaphoreType.DMA((len(pieces),)),
+        ],
+        compiler_params=pltpu.CompilerParams(vmem_limit_bytes=VMEM),
+        cost_estimate=pl.CostEstimate(
+            flops=2 * rows * cols * width,
+            bytes_accessed=2 * cols * width,
+            transcendentals=0,
+        ),
+        name=name,
+    )(*xs, *ss, w, *(() if add is None else (add,)))
+
+
+def after(value, *first):
+    anywhere = pl.BlockSpec(memory_space=pl.ANY)
+    return pl.pallas_call(
+        lambda *refs: None,
+        out_shape=jax.ShapeDtypeStruct(value.shape, value.dtype),
+        in_specs=[anywhere] * (1 + len(first)),
+        out_specs=anywhere,
+        input_output_aliases={0: 0},
+        compiler_params=pltpu.CompilerParams(vmem_limit_bytes=SMALL),
+        name="after",
+    )(value, *first)
+
+
+def line_of_four(codes, token_scale, weight_codes, weight_scale, smoothing):
+    rows, depth = codes.shape
+    bf16, f32 = jnp.bfloat16, jnp.float32
+    cut = (depth // LANES * 34 // 52) * LANES
+    spans = [(0, cut), (cut, depth - cut)]
+
+    def send(value, pairs):
+        return lax.ppermute(value, "batch", pairs)
+
+    def parts(value):
+        return [lax.slice_in_dim(value, a, a + n, axis=1) for a, n in spans]
+
+    a1 = send(codes, OUTER)
+    b1 = send(codes, INNER)
+    scales = smoothing[None, :]
+    scales = [scales] + [
+        send(scales, [(i, (i + k) % 4) for i in range(4)]) for k in (1, 2, 3)
+    ]
+    e2 = send(b1, ENDS)
+    b2 = [send(v, INNER) for v in parts(a1)]
+
+    def either(inner, outer, x_v, row, sem):
+        z = lax.axis_index("batch")
+        is_outer = (z == 0) | (z == 3)
+        here = x_v.at[pl.ds(row, rows)]
+
+        @pl.when(is_outer)
+        def _():
+            pltpu.make_async_copy(outer, here, sem).start()
+
+        @pl.when(jnp.logical_not(is_outer))
+        def _():
+            pltpu.make_async_copy(inner, here, sem).start()
+
+        return pltpu.make_async_copy(inner, here, sem).wait
+
+    def place_pair(xs, x_v, sem):
+        own_ref, a1_ref = xs
+        mine = lax.rem(lax.axis_index("batch") + lax.axis_index("mp"), 2) == 0
+        at = jnp.where(mine, 0, rows)
+        copies = [
+            pltpu.make_async_copy(
+                ref, x_v.at[pl.ds(pl.multiple_of(to, rows), rows)], sem.at[i]
+            )
+            for i, (ref, to) in enumerate(((own_ref, at), (a1_ref, rows - at)))
+        ]
+        for copy in copies:
+            copy.start()
+
+        def wait():
+            for copy in copies:
+                copy.wait()
+
+        return wait
+
+    def place_late(span):
+        def place(xs, x_v, sem):
+            b1_ref, e2_ref, b2_ref, e3_ref = xs
+            flip = lax.axis_index("batch") // 2 + lax.axis_index("mp")
+            at = pl.multiple_of(jnp.where(lax.rem(flip, 2) == 0, 0, rows), rows)
+            cols = (slice(None), pl.ds(*span))
+            wait_2 = either(b1_ref.at[cols], e2_ref.at[cols], x_v, at, sem.at[0])
+            at = pl.multiple_of(rows - at, rows)
+            wait_3 = either(b2_ref, e3_ref, x_v, at, sem.at[1])
+
+            def wait():
+                wait_2()
+                wait_3()
+
+            return wait
+
+        return place
+
+    two = [rows, rows]
+    w = weight_codes
+    mine, other = mm(place_pair, [codes, a1], scales, w, 0, depth, two, bf16, name="mm_early")
+    b2 = [after(b2[0], *scales[1:], e2), after(b2[1], mine, e2)]
+    e3 = [send(v, ENDS) for v in b2]
+    (ca, na), (cb, nb) = spans
+    (acc,) = mm(
+        place_late(spans[0]), [b1, e2, b2[0], e3[0]], scales, w, ca, na,
+        [2 * rows], f32, name="mm_late",
+    )
+    mine_late, other_late = mm(
+        place_late(spans[1]), [b1, e2, b2[1], e3[1]], scales, w, cb, nb,
+        two, bf16, add=acc, name="mm_last",
+    )
+
+    z, j = lax.axis_index("batch"), lax.axis_index("mp")
+
+    def flip(value, by):
+        return lax.ppermute(value, "mp", [(i, i ^ by) for i in range(4)])
+
+    swapped = flip(jnp.concatenate([other, other_late]), 1).astype(f32)
+    early = mine.astype(f32) + swapped[:rows]
+    late = mine_late.astype(f32) + swapped[rows:]
+    first_here = z // 2 == j // 2
+    kept = jnp.where(first_here, early, late)
+    sent = jnp.where(first_here, late, early).astype(bf16)
+    total = kept + flip(sent, 2).astype(f32)
+    scaled = total * token_scale[:, None] * weight_scale[None, :]
+    return scaled.astype(bf16)
+
+
 def solution(mesh):
+    fits = mesh.shape["batch"] == 4 and mesh.shape["mp"] == 4
+    per_device = line_of_four if fits else general
     in_specs = (
         P(("groups", "batch"), "mp"),
         P(("groups", "mp")),

time: 133 us -> 86.1 us (0.65)
  waiting for transfers between devices: 87.5 us -> 41.4 us
  starting transfers between devices: 0.04 us -> 20.8 us
  Pallas kernels: 0 us -> 20.4 us
  blocking collectives: 14.8 us -> 0 us
  matrix products: 14.4 us -> 0 us
  between operations: 13.4 us -> 0.19 us
    all_gather x1 -> x0, waiting for transfers between devices: 56.6 us -> none  [per_device(): lax.all_gather(codes, 'batch', axis=0, tiled=True).astype(jnp.float32)]
    ppermute x0 -> x12, waiting for transfers between devices: none -> 41.4 us  [the longest x10 32.7 us: send(): return lax.ppermute(value, 'batch', pairs)]
    reduce_scatter x1 -> x0, waiting for transfers between devices: 30.2 us -> none  [per_device(): lax.psum_scatter(partial_value, 'mp', scatter_dimension=0, tiled=True)]
    ppermute x0 -> x12, starting transfers between devices: none -> 20.8 us  [the longest x10 19.1 us: send(): return lax.ppermute(value, 'batch', pairs)]
    pallas_call x0 -> x5, Pallas kernels: none -> 20.4 us  [the longest x3 20.4 us: mm(): pl.pallas_call(body, out_shape=[jax.ShapeDtypeStruct((r, width), out_type...]
    all_gather x1 -> x0, blocking collectives: 14.8 us -> none  [per_device(): factors = lax.all_gather(smoothing, 'batch', axis=0, tiled=True)]
    dot_general x1 -> x0, matrix products: 14.4 us -> none  [per_device(): jnp.dot((lax.all_gather(codes, 'batch', axis=0, tiled=True).astype(jnp.fl...]
  transfers between devices with their start and end apart: 2 -> 12, of which waited for: 2 -> 7; matrix products, arithmetic and copies ran while one was open for 1% -> 1% of each run, Pallas kernels for 0% -> 19%
where the time goes in v1:
time: 86.1 us; the launch traced here: 85.8 us
  waiting for transfers between devices  41.4 us (48%)
  starting transfers between devices  20.8 us (24%)
  Pallas kernels  20.4 us (24%)
  local copies, waits for them, and re-layouts  1.93 us (2%)
  other arithmetic  1.13 us (1%)
    ppermute x10, waiting for transfers between devices, send(): return lax.ppermute(value, 'batch', pairs)  32.7 us
    pallas_call x3, Pallas kernels, mm(): pl.pallas_call(body, out_shape=[jax.ShapeDtypeStruct((r, width), out_type...  20.4 us
    ppermute x10, starting transfers between devices, send(): return lax.ppermute(value, 'batch', pairs)  19.1 us
    ppermute x2, waiting for transfers between devices, flip(): return lax.ppermute(value, 'mp', [(i, i ^ by) for i in range(4)])  8.74 us
  transfers between devices with their start and end apart: 12, of which 7 were waited for; matrix products, arithmetic and copies ran while one was open for 1% of the time, Pallas kernels for 19%

profile of v1, /device:TPU:0, one launch (start us, length us, event | category | flops | bytes accessed | tf_op | source)
XLA Modules:
  0.0 85.8 jit_solution(10008712536660893511)
XLA Ops:
  0.0 0.7 collective-permute-start.4
  0.7 5.9 %collective-permute-start = (bf16[64,6656]{1,0:T(8,128)(2,1)}, bf16[64,6656]{1,0:T(8,128)(2,1)S(1)}, u32[]{:S(2)}, u32[]{:S(2)}) collective-permute-start(bf16[64,6656]{1,0:T(8,128)(2,1)} %refs_0_.1), channel_id=1, source_target_pairs={{0,4},{4,0},{8,12},{12,8},{1,5},{5,1},{9,13},{13,9},{2,6},{6,2},{1... | collective-permute-start | bytes 2555912 | tf_op jit(solution)/shard_map/ppermute | solution.py:153
  6.6 1.3 %collective-permute-start.5 = (bf16[64,6656]{1,0:T(8,128)(2,1)S(1)}, bf16[64,6656]{1,0:T(8,128)(2,1)S(1)}, u32[]{:S(2)}, u32[]{:S(2)}) collective-permute-start(bf16[64,6656]{1,0:T(8,128)(2,1)S(1)} %collective-permute-done.4.refs_0_), channel_id=1, source_target_pairs={{4,0},{8,12},{5,1},{9,13},{6,2},{10,14},{7,3},{11,15},{20,16},{24,... | collective-permute-start | bytes 2555912 | tf_op jit(solution)/shard_map/ppermute | solution.py:153
  7.9 17.6 %collective-permute-done.refs_1_ = bf16[64,6656]{1,0:T(8,128)(2,1)S(1)} collective-permute-done((bf16[64,6656]{1,0:T(8,128)(2,1)}, bf16[64,6656]{1,0:T(8,128)(2,1)S(1)}, u32[]{:S(2)}, u32[]{:S(2)}) %collective-permute-start) | collective-permute-done | bytes 852000 | tf_op jit(solution)/shard_map/ppermute | solution.py:153
  25.5 0.7 collective-permute-start.8
  26.2 0.7 broadcast_in_dim.2.refs_2_.refs_4_
  26.9 4.5 %collective-permute-start.1 = (f32[1,1664]{1,0:T(1,128)S(1)}, f32[1,1664]{1,0:T(1,128)S(1)}, u32[]{:S(2)}, u32[]{:S(2)}) collective-permute-start(f32[1,1664]{1,0:T(1,128)S(1)} %broadcast_in_dim.2.refs_2_.refs_4_), channel_id=1, source_target_pairs={{0,4},{4,8},{8,12},{12,0},{1,5},{5,9},{9,13},{13,1},{2,6},{6,10},{... | collective-permute-start | bytes 19976 | tf_op jit(solution)/shard_map/ppermute | solution.py:153
  31.4 2.8 %collective-permute-start.3 = (f32[1,1664]{1,0:T(1,128)S(1)}, f32[1,1664]{1,0:T(1,128)S(1)}, u32[]{:S(2)}, u32[]{:S(2)}) collective-permute-start(f32[1,1664]{1,0:T(1,128)S(1)} %broadcast_in_dim.2.refs_2_.refs_4_), channel_id=1, source_target_pairs={{0,12},{4,0},{8,4},{12,8},{1,13},{5,1},{9,5},{13,9},{2,14},{6,2},{... | collective-permute-start | bytes 19976 | tf_op jit(solution)/shard_map/ppermute | solution.py:153
  34.2 8.4 %collective-permute-done.2.refs_4_.refs_2_.refs_6_ = f32[1,1664]{1,0:T(1,128)S(1)} collective-permute-done((f32[1,1664]{1,0:T(1,128)S(1)}, f32[1,1664]{1,0:T(1,128)S(1)}, u32[]{:S(2)}, u32[]{:S(2)}) %collective-permute-start.2) | collective-permute-done | bytes 6688 | tf_op jit(solution)/shard_map/ppermute | solution.py:153
  42.6 2.9 %collective-permute-done.3.refs_5_.refs_3_.refs_7_ = f32[1,1664]{1,0:T(1,128)S(1)} collective-permute-done((f32[1,1664]{1,0:T(1,128)S(1)}, f32[1,1664]{1,0:T(1,128)S(1)}, u32[]{:S(2)}, u32[]{:S(2)}) %collective-permute-start.3) | collective-permute-done | bytes 6688 | tf_op jit(solution)/shard_map/ppermute | solution.py:153
  45.6 1.3 %collective-permute-start.9 = (bf16[64,4352]{1,0:T(8,128)(2,1)S(1)}, bf16[64,4352]{1,0:T(8,128)(2,1)S(1)}, u32[]{:S(2)}, u32[]{:S(2)}) collective-permute-start(bf16[64,4352]{1,0:T(8,128)(2,1)S(1)} %after.3.refs_2_), channel_id=1, source_target_pairs={{4,0},{8,12},{5,1},{9,13},{6,2},{10,14},{7,3},{11,15},{20,16},{24,... | collective-permute-start | bytes 1671176 | tf_op jit(solution)/shard_map/ppermute | solution.py:153
  46.9 0.7 collective-permute-start.6
  47.6 1.1 %copy-done = bf16[64,6656]{1,0:T(8,128)(2,1)S(1)} copy-done((bf16[64,6656]{1,0:T(8,128)(2,1)S(1)}, bf16[64,6656]{1,0:T(8,128)(2,1)}, u32[]{:S(2)}) %copy-start) | copy-done | bytes 851992
  48.7 9.5 %mm_early.1 = (bf16[64,2048]{1,0:T(8,128)(2,1)S(1)}, bf16[64,2048]{1,0:T(8,128)(2,1)S(1)}) custom-call(bf16[64,6656]{1,0:T(8,128)(2,1)S(1)} %copy-done, bf16[64,6656]{1,0:T(8,128)(2,1)S(1)} %collective-permute-done.refs_1_, f32[1,1664]{1,0:T(1,128)S(1)} %broadcast_in_dim.2.refs_2_.refs_4_, f32[1,1664]{1,0:T(1,128)S(1)} %collective-permute-done.1.refs_3_.refs_1_.refs_5_, ...), custom_call_target="tpu_custom_call" | custom-call | flops 3489660928 | bytes 27262976 | tf_op jit(solution)/shard_map/mm_early/pallas_call | solution.py:109
  58.3 1.3 %collective-permute-start.7 = (bf16[64,2304]{1,0:T(8,128)(2,1)S(1)}, bf16[64,2304]{1,0:T(8,128)(2,1)S(1)}, u32[]{:S(2)}, u32[]{:S(2)}) collective-permute-start(bf16[64,2304]{1,0:T(8,128)(2,1)S(1)} %after.2.refs_2_), channel_id=1, source_target_pairs={{4,0},{8,12},{5,1},{9,13},{6,2},{10,14},{7,3},{11,15},{20,16},{24,... | collective-permute-start | bytes 884744 | tf_op jit(solution)/shard_map/ppermute | solution.py:153
  59.6 0.8 collective-permute-done.9.refs_3_
  60.3 6.7 %mm_late.1.refs_9_ = f32[128,2048]{1,0:T(8,128)S(1)} custom-call(bf16[64,6656]{1,0:T(8,128)(2,1)S(1)} %collective-permute-done.4.refs_0_, bf16[64,6656]{1,0:T(8,128)(2,1)S(1)} %collective-permute-done.5.refs_2_.refs_4_.refs_1_, bf16[64,4352]{1,0:T(8,128)(2,1)S(1)} %after.3.refs_2_, bf16[64,4352]{1,0:T(8,128)(2,1)S(1)} %collective-permute-done.9.refs_3_, ...), custom_call_target="tpu_custom_call" | custom-call | flops 2281701376 | bytes 17825792 | tf_op jit(solution)/shard_map/mm_late/pallas_call | solution.py:109
  67.0 3.0 %collective-permute-done.7.refs_3_ = bf16[64,2304]{1,0:T(8,128)(2,1)S(1)} collective-permute-done((bf16[64,2304]{1,0:T(8,128)(2,1)S(1)}, bf16[64,2304]{1,0:T(8,128)(2,1)S(1)}, u32[]{:S(2)}, u32[]{:S(2)}) %collective-permute-start.7) | collective-permute-done | bytes 294944 | tf_op jit(solution)/shard_map/ppermute | solution.py:153
  70.0 4.2 %mm_last.1 = (bf16[64,2048]{1,0:T(8,128)(2,1)S(1)}, bf16[64,2048]{1,0:T(8,128)(2,1)S(1)}) custom-call(bf16[64,6656]{1,0:T(8,128)(2,1)S(1)} %collective-permute-done.4.refs_0_, bf16[64,6656]{1,0:T(8,128)(2,1)S(1)} %collective-permute-done.5.refs_2_.refs_4_.refs_1_, bf16[64,2304]{1,0:T(8,128)(2,1)S(1)} %after.2.refs_2_, ...), custom_call_target="tpu_custom_call" | custom-call | flops 1207959552 | bytes 9437184 | tf_op jit(solution)/shard_map/mm_last/pallas_call | solution.py:109
  74.4 1.9 %collective-permute-done.10 = bf16[128,2048]{1,0:T(8,128)(2,1)S(1)} collective-permute-done((bf16[128,2048]{1,0:T(8,128)(2,1)S(1)}, bf16[128,2048]{1,0:T(8,128)(2,1)S(1)}, u32[]{:S(2)}, u32[]{:S(2)}) %collective-permute-start.10) | collective-permute-done | bytes 524320 | tf_op jit(solution)/shard_map/ppermute | solution.py:237
  76.4 0.1 select_convert_fusion
  76.5 1.5 %collective-permute-start.11 = (bf16[64,2048]{1,0:T(8,128)(2,1)S(1)}, bf16[64,2048]{1,0:T(8,128)(2,1)S(1)}, u32[]{:S(2)}, u32[]{:S(2)}) collective-permute-start(bf16[64,2048]{1,0:T(8,128)(2,1)S(1)} %select_convert_fusion), channel_id=1, source_target_pairs={{0,2},{1,3},{2,0},{3,1},{4,6},{5,7},{6,4},{7,5},{8,10},{9,11},{10,... | collective-permute-start | bytes 786440 | tf_op jit(solution)/shard_map/ppermute | solution.py:237
  78.0 6.9 %collective-permute-done.11 = bf16[64,2048]{1,0:T(8,128)(2,1)S(1)} collective-permute-done((bf16[64,2048]{1,0:T(8,128)(2,1)S(1)}, bf16[64,2048]{1,0:T(8,128)(2,1)S(1)}, u32[]{:S(2)}, u32[]{:S(2)}) %collective-permute-start.11) | collective-permute-done | bytes 262176 | tf_op jit(solution)/shard_map/ppermute | solution.py:237
  84.9 0.9 %multiply_convert_fusion = bf16[64,2048]{1,0:T(8,128)(2,1)} fusion(bf16[64,2048]{1,0:T(8,128)(2,1)S(1)} %collective-permute-done.11, f32[128,2048]{1,0:T(8,128)S(1)} %convert_element_type.19, bf16[64,2048]{1,0:T(8,128)(2,1)S(1)} %get-tuple-element.9.refs_1_, bf16[64,2048]{1,0:T(8,128)(2,1)S(1)} %get-tuple-element.12, f32[2048]{0:T(1024)S(1)} %copy-done.1, ...), kind=kLoop, calls=%fused_computation.3 | loop fusion | flops 1310720 | bytes 2105601 | tf_op jit(solution)/shard_map/convert_element_type | solution.py:247
  (18 shorter events, 0.3 us)
Async XLA Ops:
  0.0 6.6 %collective-permute-start.4 = (bf16[64,6656]{1,0:T(8,128)(2,1)}, bf16[64,6656]{1,0:T(8,128)(2,1)S(1)}, u32[]{:S(2)}, u32[]{:S(2)}) collective-permute-start(bf16[64,6656]{1,0:T(8,128)(2,1)} %refs_0_.1), channel_id=1, source_target_pairs={{4,8},{8,4},{5,9},{9,5},{6,10},{10,6},{7,11},{11,7},{20,24},{24,20... | collective-permute-start | bytes 2555912 | tf_op jit(solution)/shard_map/ppermute | solution.py:153
  0.7 24.7 %collective-permute-start = (bf16[64,6656]{1,0:T(8,128)(2,1)}, bf16[64,6656]{1,0:T(8,128)(2,1)S(1)}, u32[]{:S(2)}, u32[]{:S(2)}) collective-permute-start(bf16[64,6656]{1,0:T(8,128)(2,1)} %refs_0_.1), channel_id=1, source_target_pairs={{0,4},{4,0},{8,12},{12,8},{1,5},{5,1},{9,13},{13,9},{2,6},{6,2},{1... | collective-permute-start | bytes 2555912 | tf_op jit(solution)/shard_map/ppermute | solution.py:153
  6.6 39.0 %collective-permute-start.5 = (bf16[64,6656]{1,0:T(8,128)(2,1)S(1)}, bf16[64,6656]{1,0:T(8,128)(2,1)S(1)}, u32[]{:S(2)}, u32[]{:S(2)}) collective-permute-start(bf16[64,6656]{1,0:T(8,128)(2,1)S(1)} %collective-permute-done.4.refs_0_), channel_id=1, source_target_pairs={{4,0},{8,12},{5,1},{9,13},{6,2},{10,14},{7,3},{11,15},{20,16},{24,... | collective-permute-start | bytes 2555912 | tf_op jit(solution)/shard_map/ppermute | solution.py:153
  25.5 20.1 %collective-permute-start.8 = (bf16[64,4352]{1,0:T(8,128)(2,1)S(1)}, bf16[64,4352]{1,0:T(8,128)(2,1)S(1)}, u32[]{:S(2)}, u32[]{:S(2)}) collective-permute-start(bf16[64,4352]{1,0:T(8,128)(2,1)S(1)} %slice.17), channel_id=1, source_target_pairs={{4,8},{8,4},{5,9},{9,5},{6,10},{10,6},{7,11},{11,7},{20,24},{24,20... | collective-permute-start | bytes 1671176 | tf_op jit(solution)/shard_map/ppermute | solution.py:153
  26.9 7.3 %collective-permute-start.1 = (f32[1,1664]{1,0:T(1,128)S(1)}, f32[1,1664]{1,0:T(1,128)S(1)}, u32[]{:S(2)}, u32[]{:S(2)}) collective-permute-start(f32[1,1664]{1,0:T(1,128)S(1)} %broadcast_in_dim.2.refs_2_.refs_4_), channel_id=1, source_target_pairs={{0,4},{4,8},{8,12},{12,0},{1,5},{5,9},{9,13},{13,1},{2,6},{6,10},{... | collective-permute-start | bytes 19976 | tf_op jit(solution)/shard_map/ppermute | solution.py:153
  31.4 11.2 %collective-permute-start.2 = (f32[1,1664]{1,0:T(1,128)S(1)}, f32[1,1664]{1,0:T(1,128)S(1)}, u32[]{:S(2)}, u32[]{:S(2)}) collective-permute-start(f32[1,1664]{1,0:T(1,128)S(1)} %broadcast_in_dim.2.refs_2_.refs_4_), channel_id=1, source_target_pairs={{0,8},{4,12},{8,0},{12,4},{1,9},{5,13},{9,1},{13,5},{2,10},{6,14},... | collective-permute-start | bytes 19976 | tf_op jit(solution)/shard_map/ppermute | solution.py:153
  31.4 14.2 %collective-permute-start.3 = (f32[1,1664]{1,0:T(1,128)S(1)}, f32[1,1664]{1,0:T(1,128)S(1)}, u32[]{:S(2)}, u32[]{:S(2)}) collective-permute-start(f32[1,1664]{1,0:T(1,128)S(1)} %broadcast_in_dim.2.refs_2_.refs_4_), channel_id=1, source_target_pairs={{0,12},{4,0},{8,4},{12,8},{1,13},{5,1},{9,5},{13,9},{2,14},{6,2},{... | collective-permute-start | bytes 19976 | tf_op jit(solution)/shard_map/ppermute | solution.py:153
  45.6 14.7 %collective-permute-start.9 = (bf16[64,4352]{1,0:T(8,128)(2,1)S(1)}, bf16[64,4352]{1,0:T(8,128)(2,1)S(1)}, u32[]{:S(2)}, u32[]{:S(2)}) collective-permute-start(bf16[64,4352]{1,0:T(8,128)(2,1)S(1)} %after.3.refs_2_), channel_id=1, source_target_pairs={{4,0},{8,12},{5,1},{9,13},{6,2},{10,14},{7,3},{11,15},{20,16},{24,... | collective-permute-start | bytes 1671176 | tf_op jit(solution)/shard_map/ppermute | solution.py:153
  46.9 11.3 %collective-permute-start.6 = (bf16[64,2304]{1,0:T(8,128)(2,1)S(1)}, bf16[64,2304]{1,0:T(8,128)(2,1)S(1)}, u32[]{:S(2)}, u32[]{:S(2)}) collective-permute-start(bf16[64,2304]{1,0:T(8,128)(2,1)S(1)} %slice.16), channel_id=1, source_target_pairs={{4,8},{8,4},{5,9},{9,5},{6,10},{10,6},{7,11},{11,7},{20,24},{24,20... | collective-permute-start | bytes 884744 | tf_op jit(solution)/shard_map/ppermute | solution.py:153
  47.6 1.2 %copy-start = (bf16[64,6656]{1,0:T(8,128)(2,1)S(1)}, bf16[64,6656]{1,0:T(8,128)(2,1)}, u32[]{:S(2)}) copy-start(bf16[64,6656]{1,0:T(8,128)(2,1)} %refs_0_.1) | copy-start | bytes 2555908
  58.2 26.7 %copy-start.1 = (f32[2048]{0:T(1024)S(1)}, f32[2048]{0:T(1024)}, u32[]{:S(2)}) copy-start(f32[2048]{0:T(1024)} %param.8) | copy-start | bytes 24580
  58.3 26.6 %copy-start.2 = (f32[64]{0:T(128)S(1)}, f32[64]{0:T(128)}, u32[]{:S(2)}) copy-start(f32[64]{0:T(128)} %param.6) | copy-start | bytes 772
  58.3 11.7 %collective-permute-start.7 = (bf16[64,2304]{1,0:T(8,128)(2,1)S(1)}, bf16[64,2304]{1,0:T(8,128)(2,1)S(1)}, u32[]{:S(2)}, u32[]{:S(2)}) collective-permute-start(bf16[64,2304]{1,0:T(8,128)(2,1)S(1)} %after.2.refs_2_), channel_id=1, source_target_pairs={{4,0},{8,12},{5,1},{9,13},{6,2},{10,14},{7,3},{11,15},{20,16},{24,... | collective-permute-start | bytes 884744 | tf_op jit(solution)/shard_map/ppermute | solution.py:153
  74.3 2.0 %collective-permute-start.10 = (bf16[128,2048]{1,0:T(8,128)(2,1)S(1)}, bf16[128,2048]{1,0:T(8,128)(2,1)S(1)}, u32[]{:S(2)}, u32[]{:S(2)}) collective-permute-start(bf16[128,2048]{1,0:T(8,128)(2,1)S(1)} %pad_maximum_fusion), channel_id=1, source_target_pairs={{0,1},{1,0},{2,3},{3,2},{4,5},{5,4},{6,7},{7,6},{8,9},{9,8},{10,11... | collective-permute-start | bytes 1572872 | tf_op jit(solution)/shard_map/ppermute | solution.py:237
  76.5 8.4 %collective-permute-start.11 = (bf16[64,2048]{1,0:T(8,128)(2,1)S(1)}, bf16[64,2048]{1,0:T(8,128)(2,1)S(1)}, u32[]{:S(2)}, u32[]{:S(2)}) collective-permute-start(bf16[64,2048]{1,0:T(8,128)(2,1)S(1)} %select_convert_fusion), channel_id=1, source_target_pairs={{0,2},{1,3},{2,0},{3,1},{4,6},{5,7},{6,4},{7,5},{8,10},{9,11},{10,... | collective-permute-start | bytes 786440 | tf_op jit(solution)/shard_map/ppermute | solution.py:237

commit v2 on v1

--- a/solution.py
+++ b/solution.py
@@ -146,13 +146,13 @@
 def line_of_four(codes, token_scale, weight_codes, weight_scale, smoothing):
     rows, depth = codes.shape
     bf16, f32 = jnp.bfloat16, jnp.float32
-    cut = (depth // LANES * 34 // 52) * LANES
+    cut = (depth // LANES * 26 // 52) * LANES
     spans = [(0, cut), (cut, depth - cut)]
 
     def send(value, pairs):
         return lax.ppermute(value, "batch", pairs)
 
-    def parts(value):
+    def parts(value, spans):
         return [lax.slice_in_dim(value, a, a + n, axis=1) for a, n in spans]
 
     a1 = send(codes, OUTER)
@@ -161,23 +161,40 @@
     scales = [scales] + [
         send(scales, [(i, (i + k) % 4) for i in range(4)]) for k in (1, 2, 3)
     ]
-    e2 = send(b1, ENDS)
-    b2 = [send(v, INNER) for v in parts(a1)]
-
-    def either(inner, outer, x_v, row, sem):
+    half = (depth // LANES * 30 // 52) * LANES
+    b1 = parts(b1, [(0, half), (half, depth - half)])
+    a1 = after(a1, *scales[1:])
+    e2 = [send(v, ENDS) for v in b1]
+    b2 = [send(v, INNER) for v in parts(a1, spans)]
+
+    def either(inner, outer, x_v, row, span, sem):
         z = lax.axis_index("batch")
         is_outer = (z == 0) | (z == 3)
-        here = x_v.at[pl.ds(row, rows)]
+        runs, at = [], 0
+        for i, ref in enumerate(inner):
+            lo, hi = max(span[0], at), min(span[0] + span[1], at + ref.shape[1])
+            if lo < hi:
+                to = x_v.at[pl.ds(row, rows), pl.ds(lo - span[0], hi - lo)]
+                runs.append((i, pl.ds(lo - at, hi - lo), to))
+            at += ref.shape[1]
+
+        def copies(refs):
+            return [
+                pltpu.make_async_copy(refs[i].at[:, cols], to, sem)
+                for i, cols, to in runs
+            ]
 
         @pl.when(is_outer)
         def _():
-            pltpu.make_async_copy(outer, here, sem).start()
+            for copy in copies(outer):
+                copy.start()
 
         @pl.when(jnp.logical_not(is_outer))
         def _():
-            pltpu.make_async_copy(inner, here, sem).start()
-
-        return pltpu.make_async_copy(inner, here, sem).wait
+            for copy in copies(inner):
+                copy.start()
+
+        return [copy.wait for copy in copies(inner)]
 
     def place_pair(xs, x_v, sem):
         own_ref, a1_ref = xs
@@ -200,17 +217,15 @@
 
     def place_late(span):
         def place(xs, x_v, sem):
-            b1_ref, e2_ref, b2_ref, e3_ref = xs
             flip = lax.axis_index("batch") // 2 + lax.axis_index("mp")
             at = pl.multiple_of(jnp.where(lax.rem(flip, 2) == 0, 0, rows), rows)
-            cols = (slice(None), pl.ds(*span))
-            wait_2 = either(b1_ref.at[cols], e2_ref.at[cols], x_v, at, sem.at[0])
+            waits = either(xs[:2], xs[2:4], x_v, at, span, sem.at[0])
             at = pl.multiple_of(rows - at, rows)
-            wait_3 = either(b2_ref, e3_ref, x_v, at, sem.at[1])
+            waits += either(xs[4:5], xs[5:], x_v, at, (0, span[1]), sem.at[1])
 
             def wait():
-                wait_2()
-                wait_3()
+                for w in waits:
+                    w()
 
             return wait
 
@@ -219,15 +234,15 @@
     two = [rows, rows]
     w = weight_codes
     mine, other = mm(place_pair, [codes, a1], scales, w, 0, depth, two, bf16, name="mm_early")
-    b2 = [after(b2[0], *scales[1:], e2), after(b2[1], mine, e2)]
+    b2 = [after(b2[0], e2[0]), after(b2[1], mine, *e2)]
     e3 = [send(v, ENDS) for v in b2]
     (ca, na), (cb, nb) = spans
     (acc,) = mm(
-        place_late(spans[0]), [b1, e2, b2[0], e3[0]], scales, w, ca, na,
+        place_late(spans[0]), [*b1, *e2, b2[0], e3[0]], scales, w, ca, na,
         [2 * rows], f32, name="mm_late",
     )
     mine_late, other_late = mm(
-        place_late(spans[1]), [b1, e2, b2[1], e3[1]], scales, w, cb, nb,
+        place_late(spans[1]), [*b1, *e2, b2[1], e3[1]], scales, w, cb, nb,
         two, bf16, add=acc, name="mm_last",
     )
 

time: 86.1 us -> 80.9 us (0.940)
  waiting for transfers between devices: 41.4 us -> 38.1 us
  starting transfers between devices: 20.8 us -> 18.5 us
    ppermute x10 -> x11, waiting for transfers between devices: 32.7 us -> 29.4 us  [send(): return lax.ppermute(value, 'batch', pairs)]
    ppermute x10 -> x11, starting transfers between devices: 19.1 us -> 16.9 us  [send(): return lax.ppermute(value, 'batch', pairs)]
  transfers between devices with their start and end apart: 12 -> 13, of which waited for: 7 -> 6; matrix products, arithmetic and copies ran while one was open for 1% -> 1% of each run, Pallas kernels for 19% -> 19%
where the time goes in v2:
time: 80.9 us; the launch traced here: 80.5 us
  waiting for transfers between devices  38.1 us (47%)
  Pallas kernels  20.5 us (25%)
  starting transfers between devices  18.5 us (23%)
  local copies, waits for them, and re-layouts  1.98 us (2%)
  other arithmetic  1.13 us (1%)
    ppermute x11, waiting for transfers between devices, send(): return lax.ppermute(value, 'batch', pairs)  29.4 us
    pallas_call x3, Pallas kernels, mm(): pl.pallas_call(body, out_shape=[jax.ShapeDtypeStruct((r, width), out_type...  20.5 us
    ppermute x11, starting transfers between devices, send(): return lax.ppermute(value, 'batch', pairs)  16.9 us
    ppermute x2, waiting for transfers between devices, flip(): return lax.ppermute(value, 'mp', [(i, i ^ by) for i in range(4)])  8.73 us
    ppermute x2, starting transfers between devices, flip(): return lax.ppermute(value, 'mp', [(i, i ^ by) for i in range(4)])  1.63 us
  transfers between devices with their start and end apart: 13, of which 6 were waited for; matrix products, arithmetic and copies ran while one was open for 1% of the time, Pallas kernels for 19%

profile of v2, /device:TPU:0, one launch (start us, length us, event | category | flops | bytes accessed | tf_op | source)
XLA Modules:
  0.0 80.5 jit_solution(5650486647449501124)
XLA Ops:
  0.0 0.7 collective-permute-start.4
  0.7 5.9 %collective-permute-start = (bf16[64,6656]{1,0:T(8,128)(2,1)}, bf16[64,6656]{1,0:T(8,128)(2,1)S(1)}, u32[]{:S(2)}, u32[]{:S(2)}) collective-permute-start(bf16[64,6656]{1,0:T(8,128)(2,1)} %refs_0_.1), channel_id=1, source_target_pairs={{0,4},{4,0},{8,12},{12,8},{1,5},{5,1},{9,13},{13,9},{2,6},{6,2},{1... | collective-permute-start | bytes 2555912 | tf_op jit(solution)/shard_map/ppermute | solution.py:153
  6.6 0.7 broadcast_in_dim.2.refs_2_.refs_6_
  7.3 1.9 %collective-permute-start.2 = (f32[1,1664]{1,0:T(1,128)S(1)}, f32[1,1664]{1,0:T(1,128)S(1)}, u32[]{:S(2)}, u32[]{:S(2)}) collective-permute-start(f32[1,1664]{1,0:T(1,128)S(1)} %broadcast_in_dim.2.refs_2_.refs_6_), channel_id=1, source_target_pairs={{0,8},{4,12},{8,0},{12,4},{1,9},{5,13},{9,1},{13,5},{2,10},{6,14},... | collective-permute-start | bytes 19976 | tf_op jit(solution)/shard_map/ppermute | solution.py:153
  9.2 1.9 %collective-permute-start.3 = (f32[1,1664]{1,0:T(1,128)S(1)}, f32[1,1664]{1,0:T(1,128)S(1)}, u32[]{:S(2)}, u32[]{:S(2)}) collective-permute-start(f32[1,1664]{1,0:T(1,128)S(1)} %broadcast_in_dim.2.refs_2_.refs_6_), channel_id=1, source_target_pairs={{0,12},{4,0},{8,4},{12,8},{1,13},{5,1},{9,5},{13,9},{2,14},{6,2},{... | collective-permute-start | bytes 19976 | tf_op jit(solution)/shard_map/ppermute | solution.py:153
  11.1 1.3 %collective-permute-start.5 = (bf16[64,3840]{1,0:T(8,128)(2,1)S(1)}, bf16[64,3840]{1,0:T(8,128)(2,1)S(1)}, u32[]{:S(2)}, u32[]{:S(2)}) collective-permute-start(bf16[64,3840]{1,0:T(8,128)(2,1)S(1)} %slice.24.refs_0_), channel_id=1, source_target_pairs={{4,0},{8,12},{5,1},{9,13},{6,2},{10,14},{7,3},{11,15},{20,16},{24,... | collective-permute-start | bytes 1474568 | tf_op jit(solution)/shard_map/ppermute | solution.py:153
  12.4 14.4 %collective-permute-done.1.refs_1_.refs_3_.refs_7_ = f32[1,1664]{1,0:T(1,128)S(1)} collective-permute-done((f32[1,1664]{1,0:T(1,128)S(1)}, f32[1,1664]{1,0:T(1,128)S(1)}, u32[]{:S(2)}, u32[]{:S(2)}) %collective-permute-start.1) | collective-permute-done | bytes 6688 | tf_op jit(solution)/shard_map/ppermute | solution.py:153
  26.9 0.7 collective-permute-start.9
  27.6 0.7 collective-permute-start.7
  28.3 1.3 %collective-permute-start.6 = (bf16[64,2816]{1,0:T(8,128)(2,1)S(1)}, bf16[64,2816]{1,0:T(8,128)(2,1)S(1)}, u32[]{:S(2)}, u32[]{:S(2)}) collective-permute-start(bf16[64,2816]{1,0:T(8,128)(2,1)S(1)} %slice.25.refs_1_), channel_id=1, source_target_pairs={{4,0},{8,12},{5,1},{9,13},{6,2},{10,14},{7,3},{11,15},{20,16},{24,... | collective-permute-start | bytes 1081352 | tf_op jit(solution)/shard_map/ppermute | solution.py:153
  29.6 9.9 %collective-permute-done.5.refs_2_.refs_1_ = bf16[64,3840]{1,0:T(8,128)(2,1)S(1)} collective-permute-done((bf16[64,3840]{1,0:T(8,128)(2,1)S(1)}, bf16[64,3840]{1,0:T(8,128)(2,1)S(1)}, u32[]{:S(2)}, u32[]{:S(2)}) %collective-permute-start.5) | collective-permute-done | bytes 491552 | tf_op jit(solution)/shard_map/ppermute | solution.py:153
  39.5 1.3 %collective-permute-start.10 = (bf16[64,3328]{1,0:T(8,128)(2,1)S(1)}, bf16[64,3328]{1,0:T(8,128)(2,1)S(1)}, u32[]{:S(2)}, u32[]{:S(2)}) collective-permute-start(bf16[64,3328]{1,0:T(8,128)(2,1)S(1)} %after.5.refs_4_), channel_id=1, source_target_pairs={{4,0},{8,12},{5,1},{9,13},{6,2},{10,14},{7,3},{11,15},{20,16},{24,... | collective-permute-start | bytes 1277960 | tf_op jit(solution)/shard_map/ppermute | solution.py:153
  40.8 1.1 %copy-done = bf16[64,6656]{1,0:T(8,128)(2,1)S(1)} copy-done((bf16[64,6656]{1,0:T(8,128)(2,1)S(1)}, bf16[64,6656]{1,0:T(8,128)(2,1)}, u32[]{:S(2)}) %copy-start) | copy-done | bytes 851992
  42.0 9.5 %mm_early.1 = (bf16[64,2048]{1,0:T(8,128)(2,1)S(1)}, bf16[64,2048]{1,0:T(8,128)(2,1)S(1)}) custom-call(bf16[64,6656]{1,0:T(8,128)(2,1)S(1)} %copy-done, bf16[64,6656]{1,0:T(8,128)(2,1)S(1)} %after.3.refs_1_, f32[1,1664]{1,0:T(1,128)S(1)} %broadcast_in_dim.2.refs_2_.refs_6_, f32[1,1664]{1,0:T(1,128)S(1)} %collective-permute-done.1.refs_1_.refs_3_.refs_7_, ...), custom_call_target="tpu_custom_call" | custom-call | flops 3489660928 | bytes 27262976 | tf_op jit(solution)/shard_map/mm_early/pallas_call | solution.py:109
  51.5 1.3 %collective-permute-start.8 = (bf16[64,3328]{1,0:T(8,128)(2,1)S(1)}, bf16[64,3328]{1,0:T(8,128)(2,1)S(1)}, u32[]{:S(2)}, u32[]{:S(2)}) collective-permute-start(bf16[64,3328]{1,0:T(8,128)(2,1)S(1)} %after.4.refs_4_), channel_id=1, source_target_pairs={{4,0},{8,12},{5,1},{9,13},{6,2},{10,14},{7,3},{11,15},{20,16},{24,... | collective-permute-start | bytes 1277960 | tf_op jit(solution)/shard_map/ppermute | solution.py:153
  52.8 3.6 %collective-permute-done.10.refs_5_ = bf16[64,3328]{1,0:T(8,128)(2,1)S(1)} collective-permute-done((bf16[64,3328]{1,0:T(8,128)(2,1)S(1)}, bf16[64,3328]{1,0:T(8,128)(2,1)S(1)}, u32[]{:S(2)}, u32[]{:S(2)}) %collective-permute-start.10) | collective-permute-done | bytes 426016 | tf_op jit(solution)/shard_map/ppermute | solution.py:153
  56.4 5.5 %mm_late.1.refs_11_ = f32[128,2048]{1,0:T(8,128)S(1)} custom-call(bf16[64,3840]{1,0:T(8,128)(2,1)S(1)} %slice.24.refs_0_, bf16[64,2816]{1,0:T(8,128)(2,1)S(1)} %slice.25.refs_1_, bf16[64,3840]{1,0:T(8,128)(2,1)S(1)} %collective-permute-done.5.refs_2_.refs_1_, bf16[64,2816]{1,0:T(8,128)(2,1)S(1)} %collective-permute-done.6.refs_3_, ...), custom_call_target="tpu_custom_call" | custom-call | flops 1744830464 | bytes 13631488 | tf_op jit(solution)/shard_map/mm_late/pallas_call | solution.py:109
  61.9 1.5 %collective-permute-done.8.refs_5_ = bf16[64,3328]{1,0:T(8,128)(2,1)S(1)} collective-permute-done((bf16[64,3328]{1,0:T(8,128)(2,1)S(1)}, bf16[64,3328]{1,0:T(8,128)(2,1)S(1)}, u32[]{:S(2)}, u32[]{:S(2)}) %collective-permute-start.8) | collective-permute-done | bytes 426016 | tf_op jit(solution)/shard_map/ppermute | solution.py:153
  63.4 5.5 %mm_last.1 = (bf16[64,2048]{1,0:T(8,128)(2,1)S(1)}, bf16[64,2048]{1,0:T(8,128)(2,1)S(1)}) custom-call(bf16[64,3840]{1,0:T(8,128)(2,1)S(1)} %slice.24.refs_0_, bf16[64,2816]{1,0:T(8,128)(2,1)S(1)} %slice.25.refs_1_, bf16[64,3840]{1,0:T(8,128)(2,1)S(1)} %collective-permute-done.5.refs_2_.refs_1_, bf16[64,2816]{1,0:T(8,128)(2,1)S(1)} %collective-permute-done.6.refs_3_, ...), custom_call_target="tpu_custom_call" | custom-call | flops 1744830464 | bytes 13631488 | tf_op jit(solution)/shard_map/mm_last/pallas_call | solution.py:109
  69.1 1.9 %collective-permute-done.11 = bf16[128,2048]{1,0:T(8,128)(2,1)S(1)} collective-permute-done((bf16[128,2048]{1,0:T(8,128)(2,1)S(1)}, bf16[128,2048]{1,0:T(8,128)(2,1)S(1)}, u32[]{:S(2)}, u32[]{:S(2)}) %collective-permute-start.11) | collective-permute-done | bytes 524320 | tf_op jit(solution)/shard_map/ppermute | solution.py:252
  71.1 0.1 select_convert_fusion
  71.2 1.6 %collective-permute-start.12 = (bf16[64,2048]{1,0:T(8,128)(2,1)S(1)}, bf16[64,2048]{1,0:T(8,128)(2,1)S(1)}, u32[]{:S(2)}, u32[]{:S(2)}) collective-permute-start(bf16[64,2048]{1,0:T(8,128)(2,1)S(1)} %select_convert_fusion), channel_id=1, source_target_pairs={{0,2},{1,3},{2,0},{3,1},{4,6},{5,7},{6,4},{7,5},{8,10},{9,11},{10,... | collective-permute-start | bytes 786440 | tf_op jit(solution)/shard_map/ppermute | solution.py:252
  72.8 6.9 %collective-permute-done.12 = bf16[64,2048]{1,0:T(8,128)(2,1)S(1)} collective-permute-done((bf16[64,2048]{1,0:T(8,128)(2,1)S(1)}, bf16[64,2048]{1,0:T(8,128)(2,1)S(1)}, u32[]{:S(2)}, u32[]{:S(2)}) %collective-permute-start.12) | collective-permute-done | bytes 262176 | tf_op jit(solution)/shard_map/ppermute | solution.py:252
  79.6 0.9 %multiply_convert_fusion = bf16[64,2048]{1,0:T(8,128)(2,1)} fusion(bf16[64,2048]{1,0:T(8,128)(2,1)S(1)} %collective-permute-done.12, f32[128,2048]{1,0:T(8,128)S(1)} %convert_element_type.19, bf16[64,2048]{1,0:T(8,128)(2,1)S(1)} %get-tuple-element.9.refs_1_, bf16[64,2048]{1,0:T(8,128)(2,1)S(1)} %get-tuple-element.12, f32[2048]{0:T(1024)S(1)} %copy-done.1, ...), kind=kLoop, calls=%fused_computation.3 | loop fusion | flops 1310720 | bytes 2105601 | tf_op jit(solution)/shard_map/convert_element_type | solution.py:262
  (22 shorter events, 0.4 us)
Async XLA Ops:
  0.0 11.1 %collective-permute-start.4 = (bf16[64,6656]{1,0:T(8,128)(2,1)}, bf16[64,6656]{1,0:T(8,128)(2,1)S(1)}, u32[]{:S(2)}, u32[]{:S(2)}) collective-permute-start(bf16[64,6656]{1,0:T(8,128)(2,1)} %refs_0_.1), channel_id=1, source_target_pairs={{4,8},{8,4},{5,9},{9,5},{6,10},{10,6},{7,11},{11,7},{20,24},{24,20... | collective-permute-start | bytes 2555912 | tf_op jit(solution)/shard_map/ppermute | solution.py:153
  0.7 26.1 %collective-permute-start = (bf16[64,6656]{1,0:T(8,128)(2,1)}, bf16[64,6656]{1,0:T(8,128)(2,1)S(1)}, u32[]{:S(2)}, u32[]{:S(2)}) collective-permute-start(bf16[64,6656]{1,0:T(8,128)(2,1)} %refs_0_.1), channel_id=1, source_target_pairs={{0,4},{4,0},{8,12},{12,8},{1,5},{5,1},{9,13},{13,9},{2,6},{6,2},{1... | collective-permute-start | bytes 2555912 | tf_op jit(solution)/shard_map/ppermute | solution.py:153
  7.3 19.5 %collective-permute-start.1 = (f32[1,1664]{1,0:T(1,128)S(1)}, f32[1,1664]{1,0:T(1,128)S(1)}, u32[]{:S(2)}, u32[]{:S(2)}) collective-permute-start(f32[1,1664]{1,0:T(1,128)S(1)} %broadcast_in_dim.2.refs_2_.refs_6_), channel_id=1, source_target_pairs={{0,4},{4,8},{8,12},{12,0},{1,5},{5,9},{9,13},{13,1},{2,6},{6,10},{... | collective-permute-start | bytes 19976 | tf_op jit(solution)/shard_map/ppermute | solution.py:153
  7.3 19.5 %collective-permute-start.2 = (f32[1,1664]{1,0:T(1,128)S(1)}, f32[1,1664]{1,0:T(1,128)S(1)}, u32[]{:S(2)}, u32[]{:S(2)}) collective-permute-start(f32[1,1664]{1,0:T(1,128)S(1)} %broadcast_in_dim.2.refs_2_.refs_6_), channel_id=1, source_target_pairs={{0,8},{4,12},{8,0},{12,4},{1,9},{5,13},{9,1},{13,5},{2,10},{6,14},... | collective-permute-start | bytes 19976 | tf_op jit(solution)/shard_map/ppermute | solution.py:153
  9.2 17.6 %collective-permute-start.3 = (f32[1,1664]{1,0:T(1,128)S(1)}, f32[1,1664]{1,0:T(1,128)S(1)}, u32[]{:S(2)}, u32[]{:S(2)}) collective-permute-start(f32[1,1664]{1,0:T(1,128)S(1)} %broadcast_in_dim.2.refs_2_.refs_6_), channel_id=1, source_target_pairs={{0,12},{4,0},{8,4},{12,8},{1,13},{5,1},{9,5},{13,9},{2,14},{6,2},{... | collective-permute-start | bytes 19976 | tf_op jit(solution)/shard_map/ppermute | solution.py:153
  11.1 28.4 %collective-permute-start.5 = (bf16[64,3840]{1,0:T(8,128)(2,1)S(1)}, bf16[64,3840]{1,0:T(8,128)(2,1)S(1)}, u32[]{:S(2)}, u32[]{:S(2)}) collective-permute-start(bf16[64,3840]{1,0:T(8,128)(2,1)S(1)} %slice.24.refs_0_), channel_id=1, source_target_pairs={{4,0},{8,12},{5,1},{9,13},{6,2},{10,14},{7,3},{11,15},{20,16},{24,... | collective-permute-start | bytes 1474568 | tf_op jit(solution)/shard_map/ppermute | solution.py:153
  26.9 2.7 %collective-permute-start.9 = (bf16[64,3328]{1,0:T(8,128)(2,1)S(1)}, bf16[64,3328]{1,0:T(8,128)(2,1)S(1)}, u32[]{:S(2)}, u32[]{:S(2)}) collective-permute-start(bf16[64,3328]{1,0:T(8,128)(2,1)S(1)} %get-tuple-element.13), channel_id=1, source_target_pairs={{4,8},{8,4},{5,9},{9,5},{6,10},{10,6},{7,11},{11,7},{20,24},{24,20... | collective-permute-start | bytes 1277960 | tf_op jit(solution)/shard_map/ppermute | solution.py:153
  27.6 23.9 %collective-permute-start.7 = (bf16[64,3328]{1,0:T(8,128)(2,1)S(1)}, bf16[64,3328]{1,0:T(8,128)(2,1)S(1)}, u32[]{:S(2)}, u32[]{:S(2)}) collective-permute-start(bf16[64,3328]{1,0:T(8,128)(2,1)S(1)} %get-tuple-element.14), channel_id=1, source_target_pairs={{4,8},{8,4},{5,9},{9,5},{6,10},{10,6},{7,11},{11,7},{20,24},{24,20... | collective-permute-start | bytes 1277960 | tf_op jit(solution)/shard_map/ppermute | solution.py:153
  28.3 23.2 %collective-permute-start.6 = (bf16[64,2816]{1,0:T(8,128)(2,1)S(1)}, bf16[64,2816]{1,0:T(8,128)(2,1)S(1)}, u32[]{:S(2)}, u32[]{:S(2)}) collective-permute-start(bf16[64,2816]{1,0:T(8,128)(2,1)S(1)} %slice.25.refs_1_), channel_id=1, source_target_pairs={{4,0},{8,12},{5,1},{9,13},{6,2},{10,14},{7,3},{11,15},{20,16},{24,... | collective-permute-start | bytes 1081352 | tf_op jit(solution)/shard_map/ppermute | solution.py:153
  39.5 16.9 %collective-permute-start.10 = (bf16[64,3328]{1,0:T(8,128)(2,1)S(1)}, bf16[64,3328]{1,0:T(8,128)(2,1)S(1)}, u32[]{:S(2)}, u32[]{:S(2)}) collective-permute-start(bf16[64,3328]{1,0:T(8,128)(2,1)S(1)} %after.5.refs_4_), channel_id=1, source_target_pairs={{4,0},{8,12},{5,1},{9,13},{6,2},{10,14},{7,3},{11,15},{20,16},{24,... | collective-permute-start | bytes 1277960 | tf_op jit(solution)/shard_map/ppermute | solution.py:153
  40.8 1.2 %copy-start = (bf16[64,6656]{1,0:T(8,128)(2,1)S(1)}, bf16[64,6656]{1,0:T(8,128)(2,1)}, u32[]{:S(2)}) copy-start(bf16[64,6656]{1,0:T(8,128)(2,1)} %refs_0_.1) | copy-start | bytes 2555908
  51.5 28.1 %copy-start.1 = (f32[2048]{0:T(1024)S(1)}, f32[2048]{0:T(1024)}, u32[]{:S(2)}) copy-start(f32[2048]{0:T(1024)} %param.8) | copy-start | bytes 24580
  51.5 28.1 %copy-start.2 = (f32[64]{0:T(128)S(1)}, f32[64]{0:T(128)}, u32[]{:S(2)}) copy-start(f32[64]{0:T(128)} %param.6) | copy-start | bytes 772
  51.5 11.9 %collective-permute-start.8 = (bf16[64,3328]{1,0:T(8,128)(2,1)S(1)}, bf16[64,3328]{1,0:T(8,128)(2,1)S(1)}, u32[]{:S(2)}, u32[]{:S(2)}) collective-permute-start(bf16[64,3328]{1,0:T(8,128)(2,1)S(1)} %after.4.refs_4_), channel_id=1, source_target_pairs={{4,0},{8,12},{5,1},{9,13},{6,2},{10,14},{7,3},{11,15},{20,16},{24,... | collective-permute-start | bytes 1277960 | tf_op jit(solution)/shard_map/ppermute | solution.py:153
  69.0 2.0 %collective-permute-start.11 = (bf16[128,2048]{1,0:T(8,128)(2,1)S(1)}, bf16[128,2048]{1,0:T(8,128)(2,1)S(1)}, u32[]{:S(2)}, u32[]{:S(2)}) collective-permute-start(bf16[128,2048]{1,0:T(8,128)(2,1)S(1)} %pad_maximum_fusion), channel_id=1, source_target_pairs={{0,1},{1,0},{2,3},{3,2},{4,5},{5,4},{6,7},{7,6},{8,9},{9,8},{10,11... | collective-permute-start | bytes 1572872 | tf_op jit(solution)/shard_map/ppermute | solution.py:252
  71.2 8.4 %collective-permute-start.12 = (bf16[64,2048]{1,0:T(8,128)(2,1)S(1)}, bf16[64,2048]{1,0:T(8,128)(2,1)S(1)}, u32[]{:S(2)}, u32[]{:S(2)}) collective-permute-start(bf16[64,2048]{1,0:T(8,128)(2,1)S(1)} %select_convert_fusion), channel_id=1, source_target_pairs={{0,2},{1,3},{2,0},{3,1},{4,6},{5,7},{6,4},{7,5},{8,10},{9,11},{10,... | collective-permute-start | bytes 786440 | tf_op jit(solution)/shard_map/ppermute | solution.py:252

commit v3 on v2

--- a/solution.py
+++ b/solution.py
@@ -6,7 +6,9 @@
 from jax.sharding import PartitionSpec as P
 
 LANES = 128
-VMEM = 44 << 20
+VMEM = 36 << 20
+KEEP = 36 << 20
+FEW = 12 << 20
 SMALL = 1 << 20
 OUTER = [(0, 1), (1, 0), (2, 3), (3, 2)]
 INNER = [(1, 2), (2, 1)]
@@ -45,21 +47,28 @@
     return out
 
 
-def mm_kernel(place, first, pieces, n_x, n_s, n_after, has_add, n_out, split, *refs):
+def mm_kernel(place, first, pieces, n_x, n_s, has_w, has_add, split, keep, *refs):
     xs, refs = refs[:n_x], refs[n_x:]
     ss, refs = refs[:n_s], refs[n_s:]
-    w_hbm, refs = refs[0], refs[1 + n_after :]
+    w_in, refs = refs[0], refs[1:]
     add = None
     if has_add:
         add, refs = refs[0], refs[1:]
-    outs, refs = refs[:n_out], refs[n_out:]
-    x_v, s_v, w_v, acc, sem_x, sem_s, sem_w = refs
-    copy_w = [
-        pltpu.make_async_copy(
-            w_hbm.at[pl.ds(first + at, size)], w_v.at[pl.ds(at, size)], sem_w.at[i]
-        )
-        for i, (at, size) in enumerate(pieces)
-    ]
+    outs, refs = refs[: len(split)], refs[len(split) :]
+    if has_w:
+        w_v = w_in
+    else:
+        w_v, refs = refs[0], refs[1:]
+    x_v, s_v, acc, sem_x, sem_s, sem_w = refs
+    copy_w = []
+    if not has_w:
+        copy_w = [
+            pltpu.make_async_copy(
+                w_in.at[pl.ds(first + at, size)], w_v.at[pl.ds(at, size)], sem_w.at[i]
+            )
+            for i, (at, size) in enumerate(pieces)
+        ]
+        copy_w[0].start()
     n = ss[0].shape[1]
     z = lax.axis_index("batch")
     copy_s = [
@@ -70,7 +79,6 @@
         )
         for k, ref in enumerate(ss)
     ]
-    copy_w[0].start()
     for copy in copy_s:
         copy.start()
     wait_x = place(xs, x_v, sem_x)
@@ -83,7 +91,8 @@
         part = slice(at, at + size)
         s = s_v[:, first + at : first + at + size]
         x = (x_v[:, part].astype(jnp.float32) * s).astype(jnp.bfloat16)
-        copy_w[i].wait()
+        if copy_w:
+            copy_w[i].wait()
         y = jnp.dot(x, w_v[part, :], preferred_element_type=jnp.float32)
         if i == 0:
             acc[...] = y if add is None else y + add[...]
@@ -97,30 +106,42 @@
                 at += rows
 
 
-def mm(place, xs, ss, w, first, cols, split, out_type, add=None, name="mm"):
+def mm(
+    place, xs, ss, w, first, cols, split, out_type, add=None, keep=False, name="mm"
+):
     pieces = pieces_of(cols)
     width = w.shape[1]
     rows = sum(split)
+    has_w = w.shape[0] == cols
     body = lambda *refs: mm_kernel(
-        place, first, pieces, len(xs), len(ss), 0, add is not None, len(split), split, *refs
+        place, first, pieces, len(xs), len(ss), has_w, add is not None, split, keep, *refs
     )
     anywhere = pl.BlockSpec(memory_space=pl.ANY)
     vmem = pl.BlockSpec(memory_space=pltpu.VMEM)
+    outs = [jax.ShapeDtypeStruct((r, width), out_type) for r in split]
+    scratch = [
+        pltpu.VMEM((rows, cols), jnp.bfloat16),
+        pltpu.VMEM((1, sum(s.shape[1] for s in ss)), jnp.float32),
+        pltpu.VMEM((rows, width), jnp.float32),
+        pltpu.SemaphoreType.DMA((3,)),
+        pltpu.SemaphoreType.DMA((len(ss),)),
+        pltpu.SemaphoreType.DMA((len(pieces),)),
+    ]
+    if keep:
+        outs.append(jax.ShapeDtypeStruct((cols, width), w.dtype))
+    elif not has_w:
+        scratch.insert(0, pltpu.VMEM((cols, width), w.dtype))
     return pl.pallas_call(
         body,
-        out_shape=[jax.ShapeDtypeStruct((r, width), out_type) for r in split],
-        in_specs=[anywhere] * (len(xs) + len(ss) + 1) + ([vmem] if add is not None else []),
-        out_specs=[vmem] * len(split),
-        scratch_shapes=[
-            pltpu.VMEM((rows, cols), jnp.bfloat16),
-            pltpu.VMEM((1, sum(s.shape[1] for s in ss)), jnp.float32),
-            pltpu.VMEM((cols, width), jnp.bfloat16),
-            pltpu.VMEM((rows, width), jnp.float32),
-            pltpu.SemaphoreType.DMA((3,)),
-            pltpu.SemaphoreType.DMA((len(ss),)),
-            pltpu.SemaphoreType.DMA((len(pieces),)),
-        ],
-        compiler_params=pltpu.CompilerParams(vmem_limit_bytes=VMEM),
+        out_shape=outs,
+        in_specs=[anywhere] * (len(xs) + len(ss))
+        + [vmem if has_w else anywhere]
+        + ([vmem] if add is not None else []),
+        out_specs=[vmem] * len(outs),
+        scratch_shapes=scratch,
+        compiler_params=pltpu.CompilerParams(
+            vmem_limit_bytes=FEW if has_w else KEEP if keep else VMEM
+        ),
         cost_estimate=pl.CostEstimate(
             flops=2 * rows * cols * width,
             bytes_accessed=2 * cols * width,
@@ -196,24 +217,29 @@
 
         return [copy.wait for copy in copies(inner)]
 
-    def place_pair(xs, x_v, sem):
-        own_ref, a1_ref = xs
-        mine = lax.rem(lax.axis_index("batch") + lax.axis_index("mp"), 2) == 0
-        at = jnp.where(mine, 0, rows)
-        copies = [
-            pltpu.make_async_copy(
-                ref, x_v.at[pl.ds(pl.multiple_of(to, rows), rows)], sem.at[i]
-            )
-            for i, (ref, to) in enumerate(((own_ref, at), (a1_ref, rows - at)))
-        ]
-        for copy in copies:
-            copy.start()
-
-        def wait():
+    def place_pair(span):
+        def place(xs, x_v, sem):
+            own_ref, a1_ref = xs
+            mine = lax.rem(lax.axis_index("batch") + lax.axis_index("mp"), 2) == 0
+            at = jnp.where(mine, 0, rows)
+            copies = [
+                pltpu.make_async_copy(
+                    ref.at[:, pl.ds(*span)],
+                    x_v.at[pl.ds(pl.multiple_of(to, rows), rows)],
+                    sem.at[i],
+                )
+                for i, (ref, to) in enumerate(((own_ref, at), (a1_ref, rows - at)))
+            ]
             for copy in copies:
-                copy.wait()
-
-        return wait
+                copy.start()
+
+            def wait():
+                for copy in copies:
+                    copy.wait()
+
+            return wait
+
+        return place
 
     def place_late(span):
         def place(xs, x_v, sem):
@@ -233,16 +259,23 @@
 
     two = [rows, rows]
     w = weight_codes
-    mine, other = mm(place_pair, [codes, a1], scales, w, 0, depth, two, bf16, name="mm_early")
-    b2 = [after(b2[0], e2[0]), after(b2[1], mine, *e2)]
+    (ca, na), (cb, nb) = spans
+    (acc,) = mm(
+        place_pair(spans[0]), [codes, a1], scales, w, ca, na, [2 * rows], f32,
+        name="mm_early",
+    )
+    mine, other, w_rest = mm(
+        place_pair(spans[1]), [codes, a1], scales, w, cb, nb, two, bf16, add=acc, keep=True,
+        name="mm_early_rest",
+    )
+    b2 = [after(b2[0], e2[0], acc), after(b2[1], mine, *e2)]
     e3 = [send(v, ENDS) for v in b2]
-    (ca, na), (cb, nb) = spans
     (acc,) = mm(
         place_late(spans[0]), [*b1, *e2, b2[0], e3[0]], scales, w, ca, na,
         [2 * rows], f32, name="mm_late",
     )
     mine_late, other_late = mm(
-        place_late(spans[1]), [*b1, *e2, b2[1], e3[1]], scales, w, cb, nb,
+        place_late(spans[1]), [*b1, *e2, b2[1], e3[1]], scales, w_rest, cb, nb,
         two, bf16, add=acc, name="mm_last",
     )
 

time: 80.9 us -> 77.7 us (0.960)
  Pallas kernels: 20.5 us -> 18.8 us
  waiting for transfers between devices: 38.1 us -> 36.6 us
    pallas_call x3 -> x4, Pallas kernels: 20.5 us -> 18.8 us  [mm(): pl.pallas_call(body, out_shape=outs, in_specs=[anywhere] * (len(xs) + len...]
    ppermute x11, waiting for transfers between devices: 29.4 us -> 27.8 us  [send(): return lax.ppermute(value, 'batch', pairs)]
  transfers between devices with their start and end apart: 13 -> 13, of which waited for: 6 -> 7; matrix products, arithmetic and copies ran while one was open for 1% -> 1% of each run, Pallas kernels for 19% -> 21%
where the time goes in v3:
time: 77.7 us; the launch traced here: 77.4 us
  waiting for transfers between devices  36.6 us (47%)
  Pallas kernels  18.8 us (24%)
  starting transfers between devices  18.7 us (24%)
  local copies, waits for them, and re-layouts  1.98 us (3%)
  other arithmetic  1.13 us (1%)
    ppermute x11, waiting for transfers between devices, send(): return lax.ppermute(value, 'batch', pairs)  27.8 us
    pallas_call x4, Pallas kernels, mm(): pl.pallas_call(body, out_shape=outs, in_specs=[anywhere] * (len(xs) + len...  18.8 us
    ppermute x11, starting transfers between devices, send(): return lax.ppermute(value, 'batch', pairs)  17.1 us
    ppermute x2, waiting for transfers between devices, flip(): return lax.ppermute(value, 'mp', [(i, i ^ by) for i in range(4)])  8.73 us
    ppermute x2, starting transfers between devices, flip(): return lax.ppermute(value, 'mp', [(i, i ^ by) for i in range(4)])  1.62 us
  transfers between devices with their start and end apart: 13, of which 7 were waited for; matrix products, arithmetic and copies ran while one was open for 1% of the time, Pallas kernels for 21%

profile of v3, /device:TPU:0, one launch (start us, length us, event | category | flops | bytes accessed | tf_op | source)
XLA Modules:
  0.0 77.4 jit_solution(2881201197069211791)
XLA Ops:
  0.0 0.7 collective-permute-start.4
  0.7 5.9 %collective-permute-start = (bf16[64,6656]{1,0:T(8,128)(2,1)}, bf16[64,6656]{1,0:T(8,128)(2,1)S(1)}, u32[]{:S(2)}, u32[]{:S(2)}) collective-permute-start(bf16[64,6656]{1,0:T(8,128)(2,1)} %refs_0_.3), channel_id=1, source_target_pairs={{0,4},{4,0},{8,12},{12,8},{1,5},{5,1},{9,13},{13,9},{2,6},{6,2},{1... | collective-permute-start | bytes 2555912 | tf_op jit(solution)/shard_map/ppermute | solution.py:174
  6.6 0.7 broadcast_in_dim.2.refs_2_.refs_6_
  7.3 1.9 %collective-permute-start.2 = (f32[1,1664]{1,0:T(1,128)S(1)}, f32[1,1664]{1,0:T(1,128)S(1)}, u32[]{:S(2)}, u32[]{:S(2)}) collective-permute-start(f32[1,1664]{1,0:T(1,128)S(1)} %broadcast_in_dim.2.refs_2_.refs_6_), channel_id=1, source_target_pairs={{0,8},{4,12},{8,0},{12,4},{1,9},{5,13},{9,1},{13,5},{2,10},{6,14},... | collective-permute-start | bytes 19976 | tf_op jit(solution)/shard_map/ppermute | solution.py:174
  9.2 1.9 %collective-permute-start.3 = (f32[1,1664]{1,0:T(1,128)S(1)}, f32[1,1664]{1,0:T(1,128)S(1)}, u32[]{:S(2)}, u32[]{:S(2)}) collective-permute-start(f32[1,1664]{1,0:T(1,128)S(1)} %broadcast_in_dim.2.refs_2_.refs_6_), channel_id=1, source_target_pairs={{0,12},{4,0},{8,4},{12,8},{1,13},{5,1},{9,5},{13,9},{2,14},{6,2},{... | collective-permute-start | bytes 19976 | tf_op jit(solution)/shard_map/ppermute | solution.py:174
  11.1 1.3 %collective-permute-start.5 = (bf16[64,3840]{1,0:T(8,128)(2,1)S(1)}, bf16[64,3840]{1,0:T(8,128)(2,1)S(1)}, u32[]{:S(2)}, u32[]{:S(2)}) collective-permute-start(bf16[64,3840]{1,0:T(8,128)(2,1)S(1)} %slice.24.refs_0_), channel_id=1, source_target_pairs={{4,0},{8,12},{5,1},{9,13},{6,2},{10,14},{7,3},{11,15},{20,16},{24,... | collective-permute-start | bytes 1474568 | tf_op jit(solution)/shard_map/ppermute | solution.py:174
  12.4 14.4 %collective-permute-done.1.refs_1_.refs_3_.refs_7_ = f32[1,1664]{1,0:T(1,128)S(1)} collective-permute-done((f32[1,1664]{1,0:T(1,128)S(1)}, f32[1,1664]{1,0:T(1,128)S(1)}, u32[]{:S(2)}, u32[]{:S(2)}) %collective-permute-start.1) | collective-permute-done | bytes 6688 | tf_op jit(solution)/shard_map/ppermute | solution.py:174
  26.9 0.7 collective-permute-start.9
  28.3 1.3 %collective-permute-start.6 = (bf16[64,2816]{1,0:T(8,128)(2,1)S(1)}, bf16[64,2816]{1,0:T(8,128)(2,1)S(1)}, u32[]{:S(2)}, u32[]{:S(2)}) collective-permute-start(bf16[64,2816]{1,0:T(8,128)(2,1)S(1)} %slice.25.refs_1_), channel_id=1, source_target_pairs={{4,0},{8,12},{5,1},{9,13},{6,2},{10,14},{7,3},{11,15},{20,16},{24,... | collective-permute-start | bytes 1081352 | tf_op jit(solution)/shard_map/ppermute | solution.py:174
  29.6 1.1 %copy-done = bf16[64,6656]{1,0:T(8,128)(2,1)S(1)} copy-done((bf16[64,6656]{1,0:T(8,128)(2,1)S(1)}, bf16[64,6656]{1,0:T(8,128)(2,1)}, u32[]{:S(2)}) %copy-start) | copy-done | bytes 851992
  30.8 5.5 %mm_early.1.refs_7_.refs_2_ = f32[128,2048]{1,0:T(8,128)S(1)} custom-call(bf16[64,6656]{1,0:T(8,128)(2,1)S(1)} %copy-done, bf16[64,6656]{1,0:T(8,128)(2,1)S(1)} %after.3.refs_1_, f32[1,1664]{1,0:T(1,128)S(1)} %broadcast_in_dim.2.refs_2_.refs_6_, f32[1,1664]{1,0:T(1,128)S(1)} %collective-permute-done.1.refs_1_.refs_3_.refs_7_, ...), custom_call_target="tpu_custom_call" | custom-call | flops 1744830464 | bytes 13631488 | tf_op jit(solution)/shard_map/mm_early/pallas_call | solution.py:134
  36.2 3.3 %collective-permute-done.5.refs_2_.refs_1_ = bf16[64,3840]{1,0:T(8,128)(2,1)S(1)} collective-permute-done((bf16[64,3840]{1,0:T(8,128)(2,1)S(1)}, bf16[64,3840]{1,0:T(8,128)(2,1)S(1)}, u32[]{:S(2)}, u32[]{:S(2)}) %collective-permute-start.5) | collective-permute-done | bytes 491552 | tf_op jit(solution)/shard_map/ppermute | solution.py:174
  39.5 1.3 %collective-permute-start.10 = (bf16[64,3328]{1,0:T(8,128)(2,1)S(1)}, bf16[64,3328]{1,0:T(8,128)(2,1)S(1)}, u32[]{:S(2)}, u32[]{:S(2)}) collective-permute-start(bf16[64,3328]{1,0:T(8,128)(2,1)S(1)} %after.5.refs_4_), channel_id=1, source_target_pairs={{4,0},{8,12},{5,1},{9,13},{6,2},{10,14},{7,3},{11,15},{20,16},{24,... | collective-permute-start | bytes 1277960 | tf_op jit(solution)/shard_map/ppermute | solution.py:174
  40.8 5.5 %mm_early_rest.1 = (bf16[64,2048]{1,0:T(8,128)(2,1)S(1)}, bf16[64,2048]{1,0:T(8,128)(2,1)S(1)}, bf16[3328,2048]{1,0:T(8,128)(2,1)S(1)}) custom-call(bf16[64,6656]{1,0:T(8,128)(2,1)S(1)} %copy-done, bf16[64,6656]{1,0:T(8,128)(2,1)S(1)} %after.3.refs_1_, f32[1,1664]{1,0:T(1,128)S(1)} %broadcast_in_dim.2.refs_2_.refs_6_, ...), custom_call_target="tpu_custom_call" | custom-call | flops 1744830464 | bytes 13631488 | tf_op jit(solution)/shard_map/mm_early_rest/pallas_call | solution.py:134
  46.3 0.9 %collective-permute-done.6.refs_3_ = bf16[64,2816]{1,0:T(8,128)(2,1)S(1)} collective-permute-done((bf16[64,2816]{1,0:T(8,128)(2,1)S(1)}, bf16[64,2816]{1,0:T(8,128)(2,1)S(1)}, u32[]{:S(2)}, u32[]{:S(2)}) %collective-permute-start.6) | collective-permute-done | bytes 360480 | tf_op jit(solution)/shard_map/ppermute | solution.py:174
  47.3 1.4 %collective-permute-start.8 = (bf16[64,3328]{1,0:T(8,128)(2,1)S(1)}, bf16[64,3328]{1,0:T(8,128)(2,1)S(1)}, u32[]{:S(2)}, u32[]{:S(2)}) collective-permute-start(bf16[64,3328]{1,0:T(8,128)(2,1)S(1)} %after.4.refs_4_), channel_id=1, source_target_pairs={{4,0},{8,12},{5,1},{9,13},{6,2},{10,14},{7,3},{11,15},{20,16},{24,... | collective-permute-start | bytes 1277960 | tf_op jit(solution)/shard_map/ppermute | solution.py:174
  48.7 7.7 %collective-permute-done.10.refs_5_ = bf16[64,3328]{1,0:T(8,128)(2,1)S(1)} collective-permute-done((bf16[64,3328]{1,0:T(8,128)(2,1)S(1)}, bf16[64,3328]{1,0:T(8,128)(2,1)S(1)}, u32[]{:S(2)}, u32[]{:S(2)}) %collective-permute-start.10) | collective-permute-done | bytes 426016 | tf_op jit(solution)/shard_map/ppermute | solution.py:174
  56.4 5.5 %mm_late.1.refs_11_ = f32[128,2048]{1,0:T(8,128)S(1)} custom-call(bf16[64,3840]{1,0:T(8,128)(2,1)S(1)} %slice.24.refs_0_, bf16[64,2816]{1,0:T(8,128)(2,1)S(1)} %slice.25.refs_1_, bf16[64,3840]{1,0:T(8,128)(2,1)S(1)} %collective-permute-done.5.refs_2_.refs_1_, bf16[64,2816]{1,0:T(8,128)(2,1)S(1)} %collective-permute-done.6.refs_3_, ...), custom_call_target="tpu_custom_call" | custom-call | flops 1744830464 | bytes 13631488 | tf_op jit(solution)/shard_map/mm_late/pallas_call | solution.py:134
  61.9 1.5 %collective-permute-done.8.refs_5_ = bf16[64,3328]{1,0:T(8,128)(2,1)S(1)} collective-permute-done((bf16[64,3328]{1,0:T(8,128)(2,1)S(1)}, bf16[64,3328]{1,0:T(8,128)(2,1)S(1)}, u32[]{:S(2)}, u32[]{:S(2)}) %collective-permute-start.8) | collective-permute-done | bytes 426016 | tf_op jit(solution)/shard_map/ppermute | solution.py:174
  63.4 2.4 %mm_last.1 = (bf16[64,2048]{1,0:T(8,128)(2,1)S(1)}, bf16[64,2048]{1,0:T(8,128)(2,1)S(1)}) custom-call(bf16[64,3840]{1,0:T(8,128)(2,1)S(1)} %slice.24.refs_0_, bf16[64,2816]{1,0:T(8,128)(2,1)S(1)} %slice.25.refs_1_, bf16[64,3840]{1,0:T(8,128)(2,1)S(1)} %collective-permute-done.5.refs_2_.refs_1_, bf16[64,2816]{1,0:T(8,128)(2,1)S(1)} %collective-permute-done.6.refs_3_, ...), custom_call_target="tpu_custom_call" | custom-call | flops 1744830464 | bytes 13631488 | tf_op jit(solution)/shard_map/mm_last/pallas_call | solution.py:134
  66.0 1.9 %collective-permute-done.11 = bf16[128,2048]{1,0:T(8,128)(2,1)S(1)} collective-permute-done((bf16[128,2048]{1,0:T(8,128)(2,1)S(1)}, bf16[128,2048]{1,0:T(8,128)(2,1)S(1)}, u32[]{:S(2)}, u32[]{:S(2)}) %collective-permute-start.11) | collective-permute-done | bytes 524320 | tf_op jit(solution)/shard_map/ppermute | solution.py:285
  68.1 1.6 %collective-permute-start.12 = (bf16[64,2048]{1,0:T(8,128)(2,1)S(1)}, bf16[64,2048]{1,0:T(8,128)(2,1)S(1)}, u32[]{:S(2)}, u32[]{:S(2)}) collective-permute-start(bf16[64,2048]{1,0:T(8,128)(2,1)S(1)} %select_convert_fusion), channel_id=1, source_target_pairs={{0,2},{1,3},{2,0},{3,1},{4,6},{5,7},{6,4},{7,5},{8,10},{9,11},{10,... | collective-permute-start | bytes 786440 | tf_op jit(solution)/shard_map/ppermute | solution.py:285
  69.6 6.9 %collective-permute-done.12 = bf16[64,2048]{1,0:T(8,128)(2,1)S(1)} collective-permute-done((bf16[64,2048]{1,0:T(8,128)(2,1)S(1)}, bf16[64,2048]{1,0:T(8,128)(2,1)S(1)}, u32[]{:S(2)}, u32[]{:S(2)}) %collective-permute-start.12) | collective-permute-done | bytes 262176 | tf_op jit(solution)/shard_map/ppermute | solution.py:285
  76.5 0.9 %multiply_convert_fusion = bf16[64,2048]{1,0:T(8,128)(2,1)} fusion(bf16[64,2048]{1,0:T(8,128)(2,1)S(1)} %collective-permute-done.12, f32[128,2048]{1,0:T(8,128)S(1)} %convert_element_type.19, bf16[64,2048]{1,0:T(8,128)(2,1)S(1)} %get-tuple-element.10.refs_1_, bf16[64,2048]{1,0:T(8,128)(2,1)S(1)} %get-tuple-element.14, f32[2048]{0:T(1024)S(1)} %copy-done.1, ...), kind=kLoop, calls=%fused_computation.3 | loop fusion | flops 1310720 | bytes 2105601 | tf_op jit(solution)/shard_map/convert_element_type | solution.py:295
  (23 shorter events, 1.2 us)
Async XLA Ops:
  0.0 11.1 %collective-permute-start.4 = (bf16[64,6656]{1,0:T(8,128)(2,1)}, bf16[64,6656]{1,0:T(8,128)(2,1)S(1)}, u32[]{:S(2)}, u32[]{:S(2)}) collective-permute-start(bf16[64,6656]{1,0:T(8,128)(2,1)} %refs_0_.3), channel_id=1, source_target_pairs={{4,8},{8,4},{5,9},{9,5},{6,10},{10,6},{7,11},{11,7},{20,24},{24,20... | collective-permute-start | bytes 2555912 | tf_op jit(solution)/shard_map/ppermute | solution.py:174
  0.7 26.1 %collective-permute-start = (bf16[64,6656]{1,0:T(8,128)(2,1)}, bf16[64,6656]{1,0:T(8,128)(2,1)S(1)}, u32[]{:S(2)}, u32[]{:S(2)}) collective-permute-start(bf16[64,6656]{1,0:T(8,128)(2,1)} %refs_0_.3), channel_id=1, source_target_pairs={{0,4},{4,0},{8,12},{12,8},{1,5},{5,1},{9,13},{13,9},{2,6},{6,2},{1... | collective-permute-start | bytes 2555912 | tf_op jit(solution)/shard_map/ppermute | solution.py:174
  7.3 19.5 %collective-permute-start.1 = (f32[1,1664]{1,0:T(1,128)S(1)}, f32[1,1664]{1,0:T(1,128)S(1)}, u32[]{:S(2)}, u32[]{:S(2)}) collective-permute-start(f32[1,1664]{1,0:T(1,128)S(1)} %broadcast_in_dim.2.refs_2_.refs_6_), channel_id=1, source_target_pairs={{0,4},{4,8},{8,12},{12,0},{1,5},{5,9},{9,13},{13,1},{2,6},{6,10},{... | collective-permute-start | bytes 19976 | tf_op jit(solution)/shard_map/ppermute | solution.py:174
  7.3 19.5 %collective-permute-start.2 = (f32[1,1664]{1,0:T(1,128)S(1)}, f32[1,1664]{1,0:T(1,128)S(1)}, u32[]{:S(2)}, u32[]{:S(2)}) collective-permute-start(f32[1,1664]{1,0:T(1,128)S(1)} %broadcast_in_dim.2.refs_2_.refs_6_), channel_id=1, source_target_pairs={{0,8},{4,12},{8,0},{12,4},{1,9},{5,13},{9,1},{13,5},{2,10},{6,14},... | collective-permute-start | bytes 19976 | tf_op jit(solution)/shard_map/ppermute | solution.py:174
  9.2 17.6 %collective-permute-start.3 = (f32[1,1664]{1,0:T(1,128)S(1)}, f32[1,1664]{1,0:T(1,128)S(1)}, u32[]{:S(2)}, u32[]{:S(2)}) collective-permute-start(f32[1,1664]{1,0:T(1,128)S(1)} %broadcast_in_dim.2.refs_2_.refs_6_), channel_id=1, source_target_pairs={{0,12},{4,0},{8,4},{12,8},{1,13},{5,1},{9,5},{13,9},{2,14},{6,2},{... | collective-permute-start | bytes 19976 | tf_op jit(solution)/shard_map/ppermute | solution.py:174
  11.1 28.4 %collective-permute-start.5 = (bf16[64,3840]{1,0:T(8,128)(2,1)S(1)}, bf16[64,3840]{1,0:T(8,128)(2,1)S(1)}, u32[]{:S(2)}, u32[]{:S(2)}) collective-permute-start(bf16[64,3840]{1,0:T(8,128)(2,1)S(1)} %slice.24.refs_0_), channel_id=1, source_target_pairs={{4,0},{8,12},{5,1},{9,13},{6,2},{10,14},{7,3},{11,15},{20,16},{24,... | collective-permute-start | bytes 1474568 | tf_op jit(solution)/shard_map/ppermute | solution.py:174
  26.9 9.4 %collective-permute-start.9 = (bf16[64,3328]{1,0:T(8,128)(2,1)S(1)}, bf16[64,3328]{1,0:T(8,128)(2,1)S(1)}, u32[]{:S(2)}, u32[]{:S(2)}) collective-permute-start(bf16[64,3328]{1,0:T(8,128)(2,1)S(1)} %get-tuple-element.15), channel_id=1, source_target_pairs={{4,8},{8,4},{5,9},{9,5},{6,10},{10,6},{7,11},{11,7},{20,24},{24,20... | collective-permute-start | bytes 1277960 | tf_op jit(solution)/shard_map/ppermute | solution.py:174
  27.6 19.7 %collective-permute-start.7 = (bf16[64,3328]{1,0:T(8,128)(2,1)S(1)}, bf16[64,3328]{1,0:T(8,128)(2,1)S(1)}, u32[]{:S(2)}, u32[]{:S(2)}) collective-permute-start(bf16[64,3328]{1,0:T(8,128)(2,1)S(1)} %get-tuple-element.16), channel_id=1, source_target_pairs={{4,8},{8,4},{5,9},{9,5},{6,10},{10,6},{7,11},{11,7},{20,24},{24,20... | collective-permute-start | bytes 1277960 | tf_op jit(solution)/shard_map/ppermute | solution.py:174
  28.3 19.0 %collective-permute-start.6 = (bf16[64,2816]{1,0:T(8,128)(2,1)S(1)}, bf16[64,2816]{1,0:T(8,128)(2,1)S(1)}, u32[]{:S(2)}, u32[]{:S(2)}) collective-permute-start(bf16[64,2816]{1,0:T(8,128)(2,1)S(1)} %slice.25.refs_1_), channel_id=1, source_target_pairs={{4,0},{8,12},{5,1},{9,13},{6,2},{10,14},{7,3},{11,15},{20,16},{24,... | collective-permute-start | bytes 1081352 | tf_op jit(solution)/shard_map/ppermute | solution.py:174
  29.6 1.2 %copy-start = (bf16[64,6656]{1,0:T(8,128)(2,1)S(1)}, bf16[64,6656]{1,0:T(8,128)(2,1)}, u32[]{:S(2)}) copy-start(bf16[64,6656]{1,0:T(8,128)(2,1)} %refs_0_.3) | copy-start | bytes 2555908
  39.5 16.9 %collective-permute-start.10 = (bf16[64,3328]{1,0:T(8,128)(2,1)S(1)}, bf16[64,3328]{1,0:T(8,128)(2,1)S(1)}, u32[]{:S(2)}, u32[]{:S(2)}) collective-permute-start(bf16[64,3328]{1,0:T(8,128)(2,1)S(1)} %after.5.refs_4_), channel_id=1, source_target_pairs={{4,0},{8,12},{5,1},{9,13},{6,2},{10,14},{7,3},{11,15},{20,16},{24,... | collective-permute-start | bytes 1277960 | tf_op jit(solution)/shard_map/ppermute | solution.py:174
  47.3 29.2 %copy-start.1 = (f32[2048]{0:T(1024)S(1)}, f32[2048]{0:T(1024)}, u32[]{:S(2)}) copy-start(f32[2048]{0:T(1024)} %param.8) | copy-start | bytes 24580
  47.3 29.2 %copy-start.2 = (f32[64]{0:T(128)S(1)}, f32[64]{0:T(128)}, u32[]{:S(2)}) copy-start(f32[64]{0:T(128)} %param.6) | copy-start | bytes 772
  47.3 16.2 %collective-permute-start.8 = (bf16[64,3328]{1,0:T(8,128)(2,1)S(1)}, bf16[64,3328]{1,0:T(8,128)(2,1)S(1)}, u32[]{:S(2)}, u32[]{:S(2)}) collective-permute-start(bf16[64,3328]{1,0:T(8,128)(2,1)S(1)} %after.4.refs_4_), channel_id=1, source_target_pairs={{4,0},{8,12},{5,1},{9,13},{6,2},{10,14},{7,3},{11,15},{20,16},{24,... | collective-permute-start | bytes 1277960 | tf_op jit(solution)/shard_map/ppermute | solution.py:174
  65.9 2.0 %collective-permute-start.11 = (bf16[128,2048]{1,0:T(8,128)(2,1)S(1)}, bf16[128,2048]{1,0:T(8,128)(2,1)S(1)}, u32[]{:S(2)}, u32[]{:S(2)}) collective-permute-start(bf16[128,2048]{1,0:T(8,128)(2,1)S(1)} %pad_maximum_fusion), channel_id=1, source_target_pairs={{0,1},{1,0},{2,3},{3,2},{4,5},{5,4},{6,7},{7,6},{8,9},{9,8},{10,11... | collective-permute-start | bytes 1572872 | tf_op jit(solution)/shard_map/ppermute | solution.py:285
  68.1 8.4 %collective-permute-start.12 = (bf16[64,2048]{1,0:T(8,128)(2,1)S(1)}, bf16[64,2048]{1,0:T(8,128)(2,1)S(1)}, u32[]{:S(2)}, u32[]{:S(2)}) collective-permute-start(bf16[64,2048]{1,0:T(8,128)(2,1)S(1)} %select_convert_fusion), channel_id=1, source_target_pairs={{0,2},{1,3},{2,0},{3,1},{4,6},{5,7},{6,4},{7,5},{8,10},{9,11},{10,... | collective-permute-start | bytes 786440 | tf_op jit(solution)/shard_map/ppermute | solution.py:285

commit v4 on v3

--- a/solution.py
+++ b/solution.py
@@ -270,6 +270,8 @@
     )
     b2 = [after(b2[0], e2[0], acc), after(b2[1], mine, *e2)]
     e3 = [send(v, ENDS) for v in b2]
+    swapped = lax.ppermute(other, "mp", [(i, i ^ 1) for i in range(4)])
+    e3[0] = after(e3[0], swapped)
     (acc,) = mm(
         place_late(spans[0]), [*b1, *e2, b2[0], e3[0]], scales, w, ca, na,
         [2 * rows], f32, name="mm_late",
@@ -284,9 +286,8 @@
     def flip(value, by):
         return lax.ppermute(value, "mp", [(i, i ^ by) for i in range(4)])
 
-    swapped = flip(jnp.concatenate([other, other_late]), 1).astype(f32)
-    early = mine.astype(f32) + swapped[:rows]
-    late = mine_late.astype(f32) + swapped[rows:]
+    early = mine.astype(f32) + swapped.astype(f32)
+    late = mine_late.astype(f32) + flip(other_late, 1).astype(f32)
     first_here = z // 2 == j // 2
     kept = jnp.where(first_here, early, late)
     sent = jnp.where(first_here, late, early).astype(bf16)

time: 77.7 us -> 77.2 us (level)
    ppermute x0 -> x1, waiting for transfers between devices: none -> 1.52 us  [line_of_four(): swapped = lax.ppermute(other, 'mp', [(i, i ^ 1) for i in range(4)])]
    ppermute x11, waiting for transfers between devices: 27.8 us -> 26.4 us  [send(): return lax.ppermute(value, 'batch', pairs)]
  transfers between devices with their start and end apart: 13 -> 14, of which waited for: 7 -> 8; matrix products, arithmetic and copies ran while one was open for 1% -> 1% of each run, Pallas kernels for 21% -> 21%
where the time goes in v4:
time: 77.2 us; the launch traced here: 76.9 us
  waiting for transfers between devices  36.2 us (47%)
  Pallas kernels  18.8 us (24%)
  starting transfers between devices  18.6 us (24%)
  local copies, waits for them, and re-layouts  1.98 us (3%)
  other arithmetic  1.05 us (1%)
    ppermute x11, waiting for transfers between devices, send(): return lax.ppermute(value, 'batch', pairs)  26.4 us
    pallas_call x4, Pallas kernels, mm(): pl.pallas_call(body, out_shape=outs, in_specs=[anywhere] * (len(xs) + len...  18.8 us
    ppermute x11, starting transfers between devices, send(): return lax.ppermute(value, 'batch', pairs)  16.9 us
    ppermute x2, waiting for transfers between devices, flip(): return lax.ppermute(value, 'mp', [(i, i ^ by) for i in range(4)])  8.36 us
    ppermute x2, starting transfers between devices, flip(): return lax.ppermute(value, 'mp', [(i, i ^ by) for i in range(4)])  1.62 us
  transfers between devices with their start and end apart: 14, of which 8 were waited for; matrix products, arithmetic and copies ran while one was open for 1% of the time, Pallas kernels for 21%

profile of v4, /device:TPU:0, one launch (start us, length us, event | category | flops | bytes accessed | tf_op | source)
XLA Modules:
  0.0 76.9 jit_solution(8733982263792347399)
XLA Ops:
  0.0 0.7 collective-permute-start.5
  0.7 5.9 %collective-permute-start = (bf16[64,6656]{1,0:T(8,128)(2,1)}, bf16[64,6656]{1,0:T(8,128)(2,1)S(1)}, u32[]{:S(2)}, u32[]{:S(2)}) collective-permute-start(bf16[64,6656]{1,0:T(8,128)(2,1)} %refs_0_.3), channel_id=1, source_target_pairs={{0,4},{4,0},{8,12},{12,8},{1,5},{5,1},{9,13},{13,9},{2,6},{6,2},{1... | collective-permute-start | bytes 2555912 | tf_op jit(solution)/shard_map/ppermute | solution.py:174
  6.6 0.7 broadcast_in_dim.2.refs_2_.refs_6_
  7.3 1.9 %collective-permute-start.2 = (f32[1,1664]{1,0:T(1,128)S(1)}, f32[1,1664]{1,0:T(1,128)S(1)}, u32[]{:S(2)}, u32[]{:S(2)}) collective-permute-start(f32[1,1664]{1,0:T(1,128)S(1)} %broadcast_in_dim.2.refs_2_.refs_6_), channel_id=1, source_target_pairs={{0,8},{4,12},{8,0},{12,4},{1,9},{5,13},{9,1},{13,5},{2,10},{6,14},... | collective-permute-start | bytes 19976 | tf_op jit(solution)/shard_map/ppermute | solution.py:174
  9.2 1.9 %collective-permute-start.3 = (f32[1,1664]{1,0:T(1,128)S(1)}, f32[1,1664]{1,0:T(1,128)S(1)}, u32[]{:S(2)}, u32[]{:S(2)}) collective-permute-start(f32[1,1664]{1,0:T(1,128)S(1)} %broadcast_in_dim.2.refs_2_.refs_6_), channel_id=1, source_target_pairs={{0,12},{4,0},{8,4},{12,8},{1,13},{5,1},{9,5},{13,9},{2,14},{6,2},{... | collective-permute-start | bytes 19976 | tf_op jit(solution)/shard_map/ppermute | solution.py:174
  11.1 1.3 %collective-permute-start.6 = (bf16[64,3840]{1,0:T(8,128)(2,1)S(1)}, bf16[64,3840]{1,0:T(8,128)(2,1)S(1)}, u32[]{:S(2)}, u32[]{:S(2)}) collective-permute-start(bf16[64,3840]{1,0:T(8,128)(2,1)S(1)} %slice.16.refs_0_), channel_id=1, source_target_pairs={{4,0},{8,12},{5,1},{9,13},{6,2},{10,14},{7,3},{11,15},{20,16},{24,... | collective-permute-start | bytes 1474568 | tf_op jit(solution)/shard_map/ppermute | solution.py:174
  12.4 14.4 %collective-permute-done.1.refs_1_.refs_3_.refs_7_ = f32[1,1664]{1,0:T(1,128)S(1)} collective-permute-done((f32[1,1664]{1,0:T(1,128)S(1)}, f32[1,1664]{1,0:T(1,128)S(1)}, u32[]{:S(2)}, u32[]{:S(2)}) %collective-permute-start.1) | collective-permute-done | bytes 6688 | tf_op jit(solution)/shard_map/ppermute | solution.py:174
  28.3 1.3 %collective-permute-start.7 = (bf16[64,2816]{1,0:T(8,128)(2,1)S(1)}, bf16[64,2816]{1,0:T(8,128)(2,1)S(1)}, u32[]{:S(2)}, u32[]{:S(2)}) collective-permute-start(bf16[64,2816]{1,0:T(8,128)(2,1)S(1)} %slice.17.refs_1_), channel_id=1, source_target_pairs={{4,0},{8,12},{5,1},{9,13},{6,2},{10,14},{7,3},{11,15},{20,16},{24,... | collective-permute-start | bytes 1081352 | tf_op jit(solution)/shard_map/ppermute | solution.py:174
  29.6 1.1 %copy-done = bf16[64,6656]{1,0:T(8,128)(2,1)S(1)} copy-done((bf16[64,6656]{1,0:T(8,128)(2,1)S(1)}, bf16[64,6656]{1,0:T(8,128)(2,1)}, u32[]{:S(2)}) %copy-start) | copy-done | bytes 851992
  30.8 5.5 %mm_early.1.refs_7_.refs_2_ = f32[128,2048]{1,0:T(8,128)S(1)} custom-call(bf16[64,6656]{1,0:T(8,128)(2,1)S(1)} %copy-done, bf16[64,6656]{1,0:T(8,128)(2,1)S(1)} %after.4.refs_1_, f32[1,1664]{1,0:T(1,128)S(1)} %broadcast_in_dim.2.refs_2_.refs_6_, f32[1,1664]{1,0:T(1,128)S(1)} %collective-permute-done.1.refs_1_.refs_3_.refs_7_, ...), custom_call_target="tpu_custom_call" | custom-call | flops 1744830464 | bytes 13631488 | tf_op jit(solution)/shard_map/mm_early/pallas_call | solution.py:134
  36.2 3.3 %collective-permute-done.6.refs_2_.refs_1_ = bf16[64,3840]{1,0:T(8,128)(2,1)S(1)} collective-permute-done((bf16[64,3840]{1,0:T(8,128)(2,1)S(1)}, bf16[64,3840]{1,0:T(8,128)(2,1)S(1)}, u32[]{:S(2)}, u32[]{:S(2)}) %collective-permute-start.6) | collective-permute-done | bytes 491552 | tf_op jit(solution)/shard_map/ppermute | solution.py:174
  39.5 1.3 %collective-permute-start.11 = (bf16[64,3328]{1,0:T(8,128)(2,1)S(1)}, bf16[64,3328]{1,0:T(8,128)(2,1)S(1)}, u32[]{:S(2)}, u32[]{:S(2)}) collective-permute-start(bf16[64,3328]{1,0:T(8,128)(2,1)S(1)} %after.6.refs_4_), channel_id=1, source_target_pairs={{4,0},{8,12},{5,1},{9,13},{6,2},{10,14},{7,3},{11,15},{20,16},{24,... | collective-permute-start | bytes 1277960 | tf_op jit(solution)/shard_map/ppermute | solution.py:174
  40.8 5.5 %mm_early_rest.1 = (bf16[64,2048]{1,0:T(8,128)(2,1)S(1)}, bf16[64,2048]{1,0:T(8,128)(2,1)S(1)}, bf16[3328,2048]{1,0:T(8,128)(2,1)S(1)}) custom-call(bf16[64,6656]{1,0:T(8,128)(2,1)S(1)} %copy-done, bf16[64,6656]{1,0:T(8,128)(2,1)S(1)} %after.4.refs_1_, f32[1,1664]{1,0:T(1,128)S(1)} %broadcast_in_dim.2.refs_2_.refs_6_, ...), custom_call_target="tpu_custom_call" | custom-call | flops 1744830464 | bytes 13631488 | tf_op jit(solution)/shard_map/mm_early_rest/pallas_call | solution.py:134
  46.3 0.9 %collective-permute-done.7.refs_3_ = bf16[64,2816]{1,0:T(8,128)(2,1)S(1)} collective-permute-done((bf16[64,2816]{1,0:T(8,128)(2,1)S(1)}, bf16[64,2816]{1,0:T(8,128)(2,1)S(1)}, u32[]{:S(2)}, u32[]{:S(2)}) %collective-permute-start.7) | collective-permute-done | bytes 360480 | tf_op jit(solution)/shard_map/ppermute | solution.py:174
  47.3 1.3 %collective-permute-start.9 = (bf16[64,3328]{1,0:T(8,128)(2,1)S(1)}, bf16[64,3328]{1,0:T(8,128)(2,1)S(1)}, u32[]{:S(2)}, u32[]{:S(2)}) collective-permute-start(bf16[64,3328]{1,0:T(8,128)(2,1)S(1)} %after.5.refs_4_), channel_id=1, source_target_pairs={{4,0},{8,12},{5,1},{9,13},{6,2},{10,14},{7,3},{11,15},{20,16},{24,... | collective-permute-start | bytes 1277960 | tf_op jit(solution)/shard_map/ppermute | solution.py:174
  48.6 1.5 %collective-permute-done.4.refs_1_ = bf16[64,2048]{1,0:T(8,128)(2,1)S(1)} collective-permute-done((bf16[64,2048]{1,0:T(8,128)(2,1)S(1)}, bf16[64,2048]{1,0:T(8,128)(2,1)S(1)}, u32[]{:S(2)}, u32[]{:S(2)}) %collective-permute-start.4) | collective-permute-done | bytes 262176 | tf_op jit(solution)/shard_map/ppermute | solution.py:273
  50.2 6.2 %collective-permute-done.11.refs_0_ = bf16[64,3328]{1,0:T(8,128)(2,1)S(1)} collective-permute-done((bf16[64,3328]{1,0:T(8,128)(2,1)S(1)}, bf16[64,3328]{1,0:T(8,128)(2,1)S(1)}, u32[]{:S(2)}, u32[]{:S(2)}) %collective-permute-start.11) | collective-permute-done | bytes 426016 | tf_op jit(solution)/shard_map/ppermute | solution.py:174
  56.4 5.5 %mm_late.1.refs_11_ = f32[128,2048]{1,0:T(8,128)S(1)} custom-call(bf16[64,3840]{1,0:T(8,128)(2,1)S(1)} %slice.16.refs_0_, bf16[64,2816]{1,0:T(8,128)(2,1)S(1)} %slice.17.refs_1_, bf16[64,3840]{1,0:T(8,128)(2,1)S(1)} %collective-permute-done.6.refs_2_.refs_1_, bf16[64,2816]{1,0:T(8,128)(2,1)S(1)} %collective-permute-done.7.refs_3_, ...), custom_call_target="tpu_custom_call" | custom-call | flops 1744830464 | bytes 13631488 | tf_op jit(solution)/shard_map/mm_late/pallas_call | solution.py:134
  61.9 1.5 %collective-permute-done.9.refs_5_ = bf16[64,3328]{1,0:T(8,128)(2,1)S(1)} collective-permute-done((bf16[64,3328]{1,0:T(8,128)(2,1)S(1)}, bf16[64,3328]{1,0:T(8,128)(2,1)S(1)}, u32[]{:S(2)}, u32[]{:S(2)}) %collective-permute-start.9) | collective-permute-done | bytes 426016 | tf_op jit(solution)/shard_map/ppermute | solution.py:174
  63.4 2.4 %mm_last.1 = (bf16[64,2048]{1,0:T(8,128)(2,1)S(1)}, bf16[64,2048]{1,0:T(8,128)(2,1)S(1)}) custom-call(bf16[64,3840]{1,0:T(8,128)(2,1)S(1)} %slice.16.refs_0_, bf16[64,2816]{1,0:T(8,128)(2,1)S(1)} %slice.17.refs_1_, bf16[64,3840]{1,0:T(8,128)(2,1)S(1)} %collective-permute-done.6.refs_2_.refs_1_, bf16[64,2816]{1,0:T(8,128)(2,1)S(1)} %collective-permute-done.7.refs_3_, ...), custom_call_target="tpu_custom_call" | custom-call | flops 1744830464 | bytes 13631488 | tf_op jit(solution)/shard_map/mm_last/pallas_call | solution.py:134
  65.9 1.5 %collective-permute-done.12 = bf16[64,2048]{1,0:T(8,128)(2,1)S(1)} collective-permute-done((bf16[64,2048]{1,0:T(8,128)(2,1)S(1)}, bf16[64,2048]{1,0:T(8,128)(2,1)S(1)}, u32[]{:S(2)}, u32[]{:S(2)}) %collective-permute-start.12) | collective-permute-done | bytes 262176 | tf_op jit(solution)/shard_map/ppermute | solution.py:287
  67.6 1.6 %collective-permute-start.13 = (bf16[64,2048]{1,0:T(8,128)(2,1)S(1)}, bf16[64,2048]{1,0:T(8,128)(2,1)S(1)}, u32[]{:S(2)}, u32[]{:S(2)}) collective-permute-start(bf16[64,2048]{1,0:T(8,128)(2,1)S(1)} %select_convert_fusion), channel_id=1, source_target_pairs={{0,2},{1,3},{2,0},{3,1},{4,6},{5,7},{6,4},{7,5},{8,10},{9,11},{10,... | collective-permute-start | bytes 786440 | tf_op jit(solution)/shard_map/ppermute | solution.py:287
  69.1 6.9 %collective-permute-done.13 = bf16[64,2048]{1,0:T(8,128)(2,1)S(1)} collective-permute-done((bf16[64,2048]{1,0:T(8,128)(2,1)S(1)}, bf16[64,2048]{1,0:T(8,128)(2,1)S(1)}, u32[]{:S(2)}, u32[]{:S(2)}) %collective-permute-start.13) | collective-permute-done | bytes 262176 | tf_op jit(solution)/shard_map/ppermute | solution.py:287
  76.0 0.9 %multiply_convert_fusion = bf16[64,2048]{1,0:T(8,128)(2,1)} fusion(bf16[64,2048]{1,0:T(8,128)(2,1)S(1)} %collective-permute-done.13, bf16[64,2048]{1,0:T(8,128)(2,1)S(1)} %collective-permute-done.4.refs_1_, bf16[64,2048]{1,0:T(8,128)(2,1)S(1)} %get-tuple-element.10.refs_1_, bf16[64,2048]{1,0:T(8,128)(2,1)S(1)} %collective-permute-done.12, ...), kind=kLoop, calls=%fused_computation | loop fusion | flops 1572864 | bytes 1581313 | tf_op jit(solution)/shard_map/convert_element_type | solution.py:296
  (24 shorter events, 1.8 us)
Async XLA Ops:
  0.0 11.1 %collective-permute-start.5 = (bf16[64,6656]{1,0:T(8,128)(2,1)}, bf16[64,6656]{1,0:T(8,128)(2,1)S(1)}, u32[]{:S(2)}, u32[]{:S(2)}) collective-permute-start(bf16[64,6656]{1,0:T(8,128)(2,1)} %refs_0_.3), channel_id=1, source_target_pairs={{4,8},{8,4},{5,9},{9,5},{6,10},{10,6},{7,11},{11,7},{20,24},{24,20... | collective-permute-start | bytes 2555912 | tf_op jit(solution)/shard_map/ppermute | solution.py:174
  0.7 26.1 %collective-permute-start = (bf16[64,6656]{1,0:T(8,128)(2,1)}, bf16[64,6656]{1,0:T(8,128)(2,1)S(1)}, u32[]{:S(2)}, u32[]{:S(2)}) collective-permute-start(bf16[64,6656]{1,0:T(8,128)(2,1)} %refs_0_.3), channel_id=1, source_target_pairs={{0,4},{4,0},{8,12},{12,8},{1,5},{5,1},{9,13},{13,9},{2,6},{6,2},{1... | collective-permute-start | bytes 2555912 | tf_op jit(solution)/shard_map/ppermute | solution.py:174
  7.3 19.5 %collective-permute-start.1 = (f32[1,1664]{1,0:T(1,128)S(1)}, f32[1,1664]{1,0:T(1,128)S(1)}, u32[]{:S(2)}, u32[]{:S(2)}) collective-permute-start(f32[1,1664]{1,0:T(1,128)S(1)} %broadcast_in_dim.2.refs_2_.refs_6_), channel_id=1, source_target_pairs={{0,4},{4,8},{8,12},{12,0},{1,5},{5,9},{9,13},{13,1},{2,6},{6,10},{... | collective-permute-start | bytes 19976 | tf_op jit(solution)/shard_map/ppermute | solution.py:174
  7.3 19.5 %collective-permute-start.2 = (f32[1,1664]{1,0:T(1,128)S(1)}, f32[1,1664]{1,0:T(1,128)S(1)}, u32[]{:S(2)}, u32[]{:S(2)}) collective-permute-start(f32[1,1664]{1,0:T(1,128)S(1)} %broadcast_in_dim.2.refs_2_.refs_6_), channel_id=1, source_target_pairs={{0,8},{4,12},{8,0},{12,4},{1,9},{5,13},{9,1},{13,5},{2,10},{6,14},... | collective-permute-start | bytes 19976 | tf_op jit(solution)/shard_map/ppermute | solution.py:174
  9.2 17.6 %collective-permute-start.3 = (f32[1,1664]{1,0:T(1,128)S(1)}, f32[1,1664]{1,0:T(1,128)S(1)}, u32[]{:S(2)}, u32[]{:S(2)}) collective-permute-start(f32[1,1664]{1,0:T(1,128)S(1)} %broadcast_in_dim.2.refs_2_.refs_6_), channel_id=1, source_target_pairs={{0,12},{4,0},{8,4},{12,8},{1,13},{5,1},{9,5},{13,9},{2,14},{6,2},{... | collective-permute-start | bytes 19976 | tf_op jit(solution)/shard_map/ppermute | solution.py:174
  11.1 28.4 %collective-permute-start.6 = (bf16[64,3840]{1,0:T(8,128)(2,1)S(1)}, bf16[64,3840]{1,0:T(8,128)(2,1)S(1)}, u32[]{:S(2)}, u32[]{:S(2)}) collective-permute-start(bf16[64,3840]{1,0:T(8,128)(2,1)S(1)} %slice.16.refs_0_), channel_id=1, source_target_pairs={{4,0},{8,12},{5,1},{9,13},{6,2},{10,14},{7,3},{11,15},{20,16},{24,... | collective-permute-start | bytes 1474568 | tf_op jit(solution)/shard_map/ppermute | solution.py:174
  26.9 9.4 %collective-permute-start.10 = (bf16[64,3328]{1,0:T(8,128)(2,1)S(1)}, bf16[64,3328]{1,0:T(8,128)(2,1)S(1)}, u32[]{:S(2)}, u32[]{:S(2)}) collective-permute-start(bf16[64,3328]{1,0:T(8,128)(2,1)S(1)} %get-tuple-element.15), channel_id=1, source_target_pairs={{4,8},{8,4},{5,9},{9,5},{6,10},{10,6},{7,11},{11,7},{20,24},{24,20... | collective-permute-start | bytes 1277960 | tf_op jit(solution)/shard_map/ppermute | solution.py:174
  27.6 19.7 %collective-permute-start.8 = (bf16[64,3328]{1,0:T(8,128)(2,1)S(1)}, bf16[64,3328]{1,0:T(8,128)(2,1)S(1)}, u32[]{:S(2)}, u32[]{:S(2)}) collective-permute-start(bf16[64,3328]{1,0:T(8,128)(2,1)S(1)} %get-tuple-element.16), channel_id=1, source_target_pairs={{4,8},{8,4},{5,9},{9,5},{6,10},{10,6},{7,11},{11,7},{20,24},{24,20... | collective-permute-start | bytes 1277960 | tf_op jit(solution)/shard_map/ppermute | solution.py:174
  28.3 19.0 %collective-permute-start.7 = (bf16[64,2816]{1,0:T(8,128)(2,1)S(1)}, bf16[64,2816]{1,0:T(8,128)(2,1)S(1)}, u32[]{:S(2)}, u32[]{:S(2)}) collective-permute-start(bf16[64,2816]{1,0:T(8,128)(2,1)S(1)} %slice.17.refs_1_), channel_id=1, source_target_pairs={{4,0},{8,12},{5,1},{9,13},{6,2},{10,14},{7,3},{11,15},{20,16},{24,... | collective-permute-start | bytes 1081352 | tf_op jit(solution)/shard_map/ppermute | solution.py:174
  29.6 1.2 %copy-start = (bf16[64,6656]{1,0:T(8,128)(2,1)S(1)}, bf16[64,6656]{1,0:T(8,128)(2,1)}, u32[]{:S(2)}) copy-start(bf16[64,6656]{1,0:T(8,128)(2,1)} %refs_0_.3) | copy-start | bytes 2555908
  39.5 16.9 %collective-permute-start.11 = (bf16[64,3328]{1,0:T(8,128)(2,1)S(1)}, bf16[64,3328]{1,0:T(8,128)(2,1)S(1)}, u32[]{:S(2)}, u32[]{:S(2)}) collective-permute-start(bf16[64,3328]{1,0:T(8,128)(2,1)S(1)} %after.6.refs_4_), channel_id=1, source_target_pairs={{4,0},{8,12},{5,1},{9,13},{6,2},{10,14},{7,3},{11,15},{20,16},{24,... | collective-permute-start | bytes 1277960 | tf_op jit(solution)/shard_map/ppermute | solution.py:174
  46.3 29.7 %copy-start.1 = (f32[2048]{0:T(1024)S(1)}, f32[2048]{0:T(1024)}, u32[]{:S(2)}) copy-start(f32[2048]{0:T(1024)} %param.8) | copy-start | bytes 24580
  46.3 29.6 %copy-start.2 = (f32[64]{0:T(128)S(1)}, f32[64]{0:T(128)}, u32[]{:S(2)}) copy-start(f32[64]{0:T(128)} %param.6) | copy-start | bytes 772
  47.3 16.2 %collective-permute-start.9 = (bf16[64,3328]{1,0:T(8,128)(2,1)S(1)}, bf16[64,3328]{1,0:T(8,128)(2,1)S(1)}, u32[]{:S(2)}, u32[]{:S(2)}) collective-permute-start(bf16[64,3328]{1,0:T(8,128)(2,1)S(1)} %after.5.refs_4_), channel_id=1, source_target_pairs={{4,0},{8,12},{5,1},{9,13},{6,2},{10,14},{7,3},{11,15},{20,16},{24,... | collective-permute-start | bytes 1277960 | tf_op jit(solution)/shard_map/ppermute | solution.py:174
  48.6 1.6 %collective-permute-start.4 = (bf16[64,2048]{1,0:T(8,128)(2,1)S(1)}, bf16[64,2048]{1,0:T(8,128)(2,1)S(1)}, u32[]{:S(2)}, u32[]{:S(2)}) collective-permute-start(bf16[64,2048]{1,0:T(8,128)(2,1)S(1)} %get-tuple-element.11), channel_id=1, source_target_pairs={{0,1},{1,0},{2,3},{3,2},{4,5},{5,4},{6,7},{7,6},{8,9},{9,8},{10,11... | collective-permute-start | bytes 786440 | tf_op jit(solution)/shard_map/ppermute | solution.py:273
  65.8 1.6 %collective-permute-start.12 = (bf16[64,2048]{1,0:T(8,128)(2,1)S(1)}, bf16[64,2048]{1,0:T(8,128)(2,1)S(1)}, u32[]{:S(2)}, u32[]{:S(2)}) collective-permute-start(bf16[64,2048]{1,0:T(8,128)(2,1)S(1)} %get-tuple-element.14), channel_id=1, source_target_pairs={{0,1},{1,0},{2,3},{3,2},{4,5},{5,4},{6,7},{7,6},{8,9},{9,8},{10,11... | collective-permute-start | bytes 786440 | tf_op jit(solution)/shard_map/ppermute | solution.py:287
  67.6 8.4 %collective-permute-start.13 = (bf16[64,2048]{1,0:T(8,128)(2,1)S(1)}, bf16[64,2048]{1,0:T(8,128)(2,1)S(1)}, u32[]{:S(2)}, u32[]{:S(2)}) collective-permute-start(bf16[64,2048]{1,0:T(8,128)(2,1)S(1)} %select_convert_fusion), channel_id=1, source_target_pairs={{0,2},{1,3},{2,0},{3,1},{4,6},{5,7},{6,4},{7,5},{8,10},{9,11},{10,... | collective-permute-start | bytes 786440 | tf_op jit(solution)/shard_map/ppermute | solution.py:287

commit v5 on v4

--- a/solution.py
+++ b/solution.py
@@ -87,6 +87,20 @@
     for copy in copy_s:
         copy.wait()
     wait_x()
+    if has_w:
+        s = s_v[:, first : first + x_v.shape[1]]
+        x_v[...] = (x_v[...].astype(jnp.float32) * s).astype(jnp.bfloat16)
+        step = w_v.shape[1] // 4
+        for c in range(0, w_v.shape[1], step):
+            part = slice(c, c + step)
+            y = jnp.dot(x_v[...], w_v[:, part], preferred_element_type=jnp.float32)
+            if add is not None:
+                y += add[:, part]
+            at = 0
+            for out, rows in zip(outs, split):
+                out[:, part] = y[at : at + rows].astype(out.dtype)
+                at += rows
+        return
     for i, (at, size) in enumerate(pieces):
         part = slice(at, at + size)
         s = s_v[:, first + at : first + at + size]
@@ -291,6 +305,7 @@
     first_here = z // 2 == j // 2
     kept = jnp.where(first_here, early, late)
     sent = jnp.where(first_here, late, early).astype(bf16)
+    kept = lax.optimization_barrier(kept)
     total = kept + flip(sent, 2).astype(f32)
     scaled = total * token_scale[:, None] * weight_scale[None, :]
     return scaled.astype(bf16)

time: 77.2 us -> 77.2 us (level)
  no operation moved by 1% of the time
where the time goes in v5:
time: 77.2 us; the launch traced here: 76.8 us
  waiting for transfers between devices  36.2 us (47%)
  Pallas kernels  18.8 us (24%)
  starting transfers between devices  18.6 us (24%)
  local copies, waits for them, and re-layouts  1.98 us (3%)
  other arithmetic  0.97 us (1%)
    ppermute x11, waiting for transfers between devices, send(): return lax.ppermute(value, 'batch', pairs)  26.4 us
    pallas_call x4, Pallas kernels, mm(): pl.pallas_call(body, out_shape=outs, in_specs=[anywhere] * (len(xs) + len...  18.8 us
    ppermute x11, starting transfers between devices, send(): return lax.ppermute(value, 'batch', pairs)  16.9 us
    ppermute x2, waiting for transfers between devices, flip(): return lax.ppermute(value, 'mp', [(i, i ^ by) for i in range(4)])  8.36 us
    ppermute x2, starting transfers between devices, flip(): return lax.ppermute(value, 'mp', [(i, i ^ by) for i in range(4)])  1.62 us
  transfers between devices with their start and end apart: 14, of which 8 were waited for; matrix products, arithmetic and copies ran while one was open for 1% of the time, Pallas kernels for 21%

profile of v5, /device:TPU:0, one launch (start us, length us, event | category | flops | bytes accessed | tf_op | source)
XLA Modules:
  0.0 76.8 jit_solution(8672648203174739534)
XLA Ops:
  0.0 0.7 collective-permute-start.5
  0.7 5.9 %collective-permute-start = (bf16[64,6656]{1,0:T(8,128)(2,1)}, bf16[64,6656]{1,0:T(8,128)(2,1)S(1)}, u32[]{:S(2)}, u32[]{:S(2)}) collective-permute-start(bf16[64,6656]{1,0:T(8,128)(2,1)} %refs_0_.3), channel_id=1, source_target_pairs={{0,4},{4,0},{8,12},{12,8},{1,5},{5,1},{9,13},{13,9},{2,6},{6,2},{1... | collective-permute-start | bytes 2555912 | tf_op jit(solution)/shard_map/ppermute | solution.py:188
  6.6 0.7 broadcast_in_dim.2.refs_2_.refs_6_
  7.3 1.9 %collective-permute-start.2 = (f32[1,1664]{1,0:T(1,128)S(1)}, f32[1,1664]{1,0:T(1,128)S(1)}, u32[]{:S(2)}, u32[]{:S(2)}) collective-permute-start(f32[1,1664]{1,0:T(1,128)S(1)} %broadcast_in_dim.2.refs_2_.refs_6_), channel_id=1, source_target_pairs={{0,8},{4,12},{8,0},{12,4},{1,9},{5,13},{9,1},{13,5},{2,10},{6,14},... | collective-permute-start | bytes 19976 | tf_op jit(solution)/shard_map/ppermute | solution.py:188
  9.2 1.9 %collective-permute-start.3 = (f32[1,1664]{1,0:T(1,128)S(1)}, f32[1,1664]{1,0:T(1,128)S(1)}, u32[]{:S(2)}, u32[]{:S(2)}) collective-permute-start(f32[1,1664]{1,0:T(1,128)S(1)} %broadcast_in_dim.2.refs_2_.refs_6_), channel_id=1, source_target_pairs={{0,12},{4,0},{8,4},{12,8},{1,13},{5,1},{9,5},{13,9},{2,14},{6,2},{... | collective-permute-start | bytes 19976 | tf_op jit(solution)/shard_map/ppermute | solution.py:188
  11.1 1.3 %collective-permute-start.6 = (bf16[64,3840]{1,0:T(8,128)(2,1)S(1)}, bf16[64,3840]{1,0:T(8,128)(2,1)S(1)}, u32[]{:S(2)}, u32[]{:S(2)}) collective-permute-start(bf16[64,3840]{1,0:T(8,128)(2,1)S(1)} %slice.16.refs_0_), channel_id=1, source_target_pairs={{4,0},{8,12},{5,1},{9,13},{6,2},{10,14},{7,3},{11,15},{20,16},{24,... | collective-permute-start | bytes 1474568 | tf_op jit(solution)/shard_map/ppermute | solution.py:188
  12.4 14.4 %collective-permute-done.1.refs_1_.refs_3_.refs_7_ = f32[1,1664]{1,0:T(1,128)S(1)} collective-permute-done((f32[1,1664]{1,0:T(1,128)S(1)}, f32[1,1664]{1,0:T(1,128)S(1)}, u32[]{:S(2)}, u32[]{:S(2)}) %collective-permute-start.1) | collective-permute-done | bytes 6688 | tf_op jit(solution)/shard_map/ppermute | solution.py:188
  28.3 1.3 %collective-permute-start.7 = (bf16[64,2816]{1,0:T(8,128)(2,1)S(1)}, bf16[64,2816]{1,0:T(8,128)(2,1)S(1)}, u32[]{:S(2)}, u32[]{:S(2)}) collective-permute-start(bf16[64,2816]{1,0:T(8,128)(2,1)S(1)} %slice.17.refs_1_), channel_id=1, source_target_pairs={{4,0},{8,12},{5,1},{9,13},{6,2},{10,14},{7,3},{11,15},{20,16},{24,... | collective-permute-start | bytes 1081352 | tf_op jit(solution)/shard_map/ppermute | solution.py:188
  29.6 1.1 %copy-done = bf16[64,6656]{1,0:T(8,128)(2,1)S(1)} copy-done((bf16[64,6656]{1,0:T(8,128)(2,1)S(1)}, bf16[64,6656]{1,0:T(8,128)(2,1)}, u32[]{:S(2)}) %copy-start) | copy-done | bytes 851992
  30.8 5.5 %mm_early.1.refs_7_.refs_2_ = f32[128,2048]{1,0:T(8,128)S(1)} custom-call(bf16[64,6656]{1,0:T(8,128)(2,1)S(1)} %copy-done, bf16[64,6656]{1,0:T(8,128)(2,1)S(1)} %after.4.refs_1_, f32[1,1664]{1,0:T(1,128)S(1)} %broadcast_in_dim.2.refs_2_.refs_6_, f32[1,1664]{1,0:T(1,128)S(1)} %collective-permute-done.1.refs_1_.refs_3_.refs_7_, ...), custom_call_target="tpu_custom_call" | custom-call | flops 1744830464 | bytes 13631488 | tf_op jit(solution)/shard_map/mm_early/pallas_call | solution.py:148
  36.2 3.3 %collective-permute-done.6.refs_2_.refs_1_ = bf16[64,3840]{1,0:T(8,128)(2,1)S(1)} collective-permute-done((bf16[64,3840]{1,0:T(8,128)(2,1)S(1)}, bf16[64,3840]{1,0:T(8,128)(2,1)S(1)}, u32[]{:S(2)}, u32[]{:S(2)}) %collective-permute-start.6) | collective-permute-done | bytes 491552 | tf_op jit(solution)/shard_map/ppermute | solution.py:188
  39.5 1.3 %collective-permute-start.11 = (bf16[64,3328]{1,0:T(8,128)(2,1)S(1)}, bf16[64,3328]{1,0:T(8,128)(2,1)S(1)}, u32[]{:S(2)}, u32[]{:S(2)}) collective-permute-start(bf16[64,3328]{1,0:T(8,128)(2,1)S(1)} %after.6.refs_4_), channel_id=1, source_target_pairs={{4,0},{8,12},{5,1},{9,13},{6,2},{10,14},{7,3},{11,15},{20,16},{24,... | collective-permute-start | bytes 1277960 | tf_op jit(solution)/shard_map/ppermute | solution.py:188
  40.8 5.5 %mm_early_rest.1 = (bf16[64,2048]{1,0:T(8,128)(2,1)S(1)}, bf16[64,2048]{1,0:T(8,128)(2,1)S(1)}, bf16[3328,2048]{1,0:T(8,128)(2,1)S(1)}) custom-call(bf16[64,6656]{1,0:T(8,128)(2,1)S(1)} %copy-done, bf16[64,6656]{1,0:T(8,128)(2,1)S(1)} %after.4.refs_1_, f32[1,1664]{1,0:T(1,128)S(1)} %broadcast_in_dim.2.refs_2_.refs_6_, ...), custom_call_target="tpu_custom_call" | custom-call | flops 1744830464 | bytes 13631488 | tf_op jit(solution)/shard_map/mm_early_rest/pallas_call | solution.py:148
  46.3 0.9 %collective-permute-done.7.refs_3_ = bf16[64,2816]{1,0:T(8,128)(2,1)S(1)} collective-permute-done((bf16[64,2816]{1,0:T(8,128)(2,1)S(1)}, bf16[64,2816]{1,0:T(8,128)(2,1)S(1)}, u32[]{:S(2)}, u32[]{:S(2)}) %collective-permute-start.7) | collective-permute-done | bytes 360480 | tf_op jit(solution)/shard_map/ppermute | solution.py:188
  47.3 1.3 %collective-permute-start.9 = (bf16[64,3328]{1,0:T(8,128)(2,1)S(1)}, bf16[64,3328]{1,0:T(8,128)(2,1)S(1)}, u32[]{:S(2)}, u32[]{:S(2)}) collective-permute-start(bf16[64,3328]{1,0:T(8,128)(2,1)S(1)} %after.5.refs_4_), channel_id=1, source_target_pairs={{4,0},{8,12},{5,1},{9,13},{6,2},{10,14},{7,3},{11,15},{20,16},{24,... | collective-permute-start | bytes 1277960 | tf_op jit(solution)/shard_map/ppermute | solution.py:188
  48.6 1.5 %collective-permute-done.4.refs_1_ = bf16[64,2048]{1,0:T(8,128)(2,1)S(1)} collective-permute-done((bf16[64,2048]{1,0:T(8,128)(2,1)S(1)}, bf16[64,2048]{1,0:T(8,128)(2,1)S(1)}, u32[]{:S(2)}, u32[]{:S(2)}) %collective-permute-start.4) | collective-permute-done | bytes 262176 | tf_op jit(solution)/shard_map/ppermute | solution.py:287
  50.2 6.2 %collective-permute-done.11.refs_0_ = bf16[64,3328]{1,0:T(8,128)(2,1)S(1)} collective-permute-done((bf16[64,3328]{1,0:T(8,128)(2,1)S(1)}, bf16[64,3328]{1,0:T(8,128)(2,1)S(1)}, u32[]{:S(2)}, u32[]{:S(2)}) %collective-permute-start.11) | collective-permute-done | bytes 426016 | tf_op jit(solution)/shard_map/ppermute | solution.py:188
  56.4 5.5 %mm_late.1.refs_11_ = f32[128,2048]{1,0:T(8,128)S(1)} custom-call(bf16[64,3840]{1,0:T(8,128)(2,1)S(1)} %slice.16.refs_0_, bf16[64,2816]{1,0:T(8,128)(2,1)S(1)} %slice.17.refs_1_, bf16[64,3840]{1,0:T(8,128)(2,1)S(1)} %collective-permute-done.6.refs_2_.refs_1_, bf16[64,2816]{1,0:T(8,128)(2,1)S(1)} %collective-permute-done.7.refs_3_, ...), custom_call_target="tpu_custom_call" | custom-call | flops 1744830464 | bytes 13631488 | tf_op jit(solution)/shard_map/mm_late/pallas_call | solution.py:148
  61.9 1.5 %collective-permute-done.9.refs_5_ = bf16[64,3328]{1,0:T(8,128)(2,1)S(1)} collective-permute-done((bf16[64,3328]{1,0:T(8,128)(2,1)S(1)}, bf16[64,3328]{1,0:T(8,128)(2,1)S(1)}, u32[]{:S(2)}, u32[]{:S(2)}) %collective-permute-start.9) | collective-permute-done | bytes 426016 | tf_op jit(solution)/shard_map/ppermute | solution.py:188
  63.4 2.4 %mm_last.1 = (bf16[64,2048]{1,0:T(8,128)(2,1)S(1)}, bf16[64,2048]{1,0:T(8,128)(2,1)S(1)}) custom-call(bf16[64,3840]{1,0:T(8,128)(2,1)S(1)} %slice.16.refs_0_, bf16[64,2816]{1,0:T(8,128)(2,1)S(1)} %slice.17.refs_1_, bf16[64,3840]{1,0:T(8,128)(2,1)S(1)} %collective-permute-done.6.refs_2_.refs_1_, bf16[64,2816]{1,0:T(8,128)(2,1)S(1)} %collective-permute-done.7.refs_3_, ...), custom_call_target="tpu_custom_call" | custom-call | flops 1744830464 | bytes 13631488 | tf_op jit(solution)/shard_map/mm_last/pallas_call | solution.py:148
  65.9 1.5 %collective-permute-done.12 = bf16[64,2048]{1,0:T(8,128)(2,1)S(1)} collective-permute-done((bf16[64,2048]{1,0:T(8,128)(2,1)S(1)}, bf16[64,2048]{1,0:T(8,128)(2,1)S(1)}, u32[]{:S(2)}, u32[]{:S(2)}) %collective-permute-start.12) | collective-permute-done | bytes 262176 | tf_op jit(solution)/shard_map/ppermute | solution.py:301
  67.6 1.6 %collective-permute-start.13 = (bf16[64,2048]{1,0:T(8,128)(2,1)S(1)}, bf16[64,2048]{1,0:T(8,128)(2,1)S(1)}, u32[]{:S(2)}, u32[]{:S(2)}) collective-permute-start(bf16[64,2048]{1,0:T(8,128)(2,1)S(1)} %get-tuple-element.15), channel_id=1, source_target_pairs={{0,2},{1,3},{2,0},{3,1},{4,6},{5,7},{6,4},{7,5},{8,10},{9,11},{10,... | collective-permute-start | bytes 786440 | tf_op jit(solution)/shard_map/ppermute | solution.py:301
  69.1 6.9 %collective-permute-done.13 = bf16[64,2048]{1,0:T(8,128)(2,1)S(1)} collective-permute-done((bf16[64,2048]{1,0:T(8,128)(2,1)S(1)}, bf16[64,2048]{1,0:T(8,128)(2,1)S(1)}, u32[]{:S(2)}, u32[]{:S(2)}) %collective-permute-start.13) | collective-permute-done | bytes 262176 | tf_op jit(solution)/shard_map/ppermute | solution.py:301
  76.0 0.8 %multiply_convert_fusion = bf16[64,2048]{1,0:T(8,128)(2,1)} fusion(f32[64,2048]{1,0:T(8,128)S(1)} %get-tuple-element.16, bf16[64,2048]{1,0:T(8,128)(2,1)S(1)} %collective-permute-done.13, f32[2048]{0:T(1024)S(1)} %copy-done.1, f32[64]{0:T(128)S(1)} %copy-done.2), kind=kLoop, calls=%fused_computation | loop fusion | flops 655360 | bytes 1057024 | tf_op jit(solution)/shard_map/convert_element_type | solution.py:311
  (24 shorter events, 1.8 us)
Async XLA Ops:
  0.0 11.1 %collective-permute-start.5 = (bf16[64,6656]{1,0:T(8,128)(2,1)}, bf16[64,6656]{1,0:T(8,128)(2,1)S(1)}, u32[]{:S(2)}, u32[]{:S(2)}) collective-permute-start(bf16[64,6656]{1,0:T(8,128)(2,1)} %refs_0_.3), channel_id=1, source_target_pairs={{4,8},{8,4},{5,9},{9,5},{6,10},{10,6},{7,11},{11,7},{20,24},{24,20... | collective-permute-start | bytes 2555912 | tf_op jit(solution)/shard_map/ppermute | solution.py:188
  0.7 26.1 %collective-permute-start = (bf16[64,6656]{1,0:T(8,128)(2,1)}, bf16[64,6656]{1,0:T(8,128)(2,1)S(1)}, u32[]{:S(2)}, u32[]{:S(2)}) collective-permute-start(bf16[64,6656]{1,0:T(8,128)(2,1)} %refs_0_.3), channel_id=1, source_target_pairs={{0,4},{4,0},{8,12},{12,8},{1,5},{5,1},{9,13},{13,9},{2,6},{6,2},{1... | collective-permute-start | bytes 2555912 | tf_op jit(solution)/shard_map/ppermute | solution.py:188
  7.3 19.5 %collective-permute-start.1 = (f32[1,1664]{1,0:T(1,128)S(1)}, f32[1,1664]{1,0:T(1,128)S(1)}, u32[]{:S(2)}, u32[]{:S(2)}) collective-permute-start(f32[1,1664]{1,0:T(1,128)S(1)} %broadcast_in_dim.2.refs_2_.refs_6_), channel_id=1, source_target_pairs={{0,4},{4,8},{8,12},{12,0},{1,5},{5,9},{9,13},{13,1},{2,6},{6,10},{... | collective-permute-start | bytes 19976 | tf_op jit(solution)/shard_map/ppermute | solution.py:188
  7.3 19.5 %collective-permute-start.2 = (f32[1,1664]{1,0:T(1,128)S(1)}, f32[1,1664]{1,0:T(1,128)S(1)}, u32[]{:S(2)}, u32[]{:S(2)}) collective-permute-start(f32[1,1664]{1,0:T(1,128)S(1)} %broadcast_in_dim.2.refs_2_.refs_6_), channel_id=1, source_target_pairs={{0,8},{4,12},{8,0},{12,4},{1,9},{5,13},{9,1},{13,5},{2,10},{6,14},... | collective-permute-start | bytes 19976 | tf_op jit(solution)/shard_map/ppermute | solution.py:188
  9.2 17.6 %collective-permute-start.3 = (f32[1,1664]{1,0:T(1,128)S(1)}, f32[1,1664]{1,0:T(1,128)S(1)}, u32[]{:S(2)}, u32[]{:S(2)}) collective-permute-start(f32[1,1664]{1,0:T(1,128)S(1)} %broadcast_in_dim.2.refs_2_.refs_6_), channel_id=1, source_target_pairs={{0,12},{4,0},{8,4},{12,8},{1,13},{5,1},{9,5},{13,9},{2,14},{6,2},{... | collective-permute-start | bytes 19976 | tf_op jit(solution)/shard_map/ppermute | solution.py:188
  11.1 28.4 %collective-permute-start.6 = (bf16[64,3840]{1,0:T(8,128)(2,1)S(1)}, bf16[64,3840]{1,0:T(8,128)(2,1)S(1)}, u32[]{:S(2)}, u32[]{:S(2)}) collective-permute-start(bf16[64,3840]{1,0:T(8,128)(2,1)S(1)} %slice.16.refs_0_), channel_id=1, source_target_pairs={{4,0},{8,12},{5,1},{9,13},{6,2},{10,14},{7,3},{11,15},{20,16},{24,... | collective-permute-start | bytes 1474568 | tf_op jit(solution)/shard_map/ppermute | solution.py:188
  26.9 9.4 %collective-permute-start.10 = (bf16[64,3328]{1,0:T(8,128)(2,1)S(1)}, bf16[64,3328]{1,0:T(8,128)(2,1)S(1)}, u32[]{:S(2)}, u32[]{:S(2)}) collective-permute-start(bf16[64,3328]{1,0:T(8,128)(2,1)S(1)} %get-tuple-element.17), channel_id=1, source_target_pairs={{4,8},{8,4},{5,9},{9,5},{6,10},{10,6},{7,11},{11,7},{20,24},{24,20... | collective-permute-start | bytes 1277960 | tf_op jit(solution)/shard_map/ppermute | solution.py:188
  27.6 19.7 %collective-permute-start.8 = (bf16[64,3328]{1,0:T(8,128)(2,1)S(1)}, bf16[64,3328]{1,0:T(8,128)(2,1)S(1)}, u32[]{:S(2)}, u32[]{:S(2)}) collective-permute-start(bf16[64,3328]{1,0:T(8,128)(2,1)S(1)} %get-tuple-element.18), channel_id=1, source_target_pairs={{4,8},{8,4},{5,9},{9,5},{6,10},{10,6},{7,11},{11,7},{20,24},{24,20... | collective-permute-start | bytes 1277960 | tf_op jit(solution)/shard_map/ppermute | solution.py:188
  28.3 19.0 %collective-permute-start.7 = (bf16[64,2816]{1,0:T(8,128)(2,1)S(1)}, bf16[64,2816]{1,0:T(8,128)(2,1)S(1)}, u32[]{:S(2)}, u32[]{:S(2)}) collective-permute-start(bf16[64,2816]{1,0:T(8,128)(2,1)S(1)} %slice.17.refs_1_), channel_id=1, source_target_pairs={{4,0},{8,12},{5,1},{9,13},{6,2},{10,14},{7,3},{11,15},{20,16},{24,... | collective-permute-start | bytes 1081352 | tf_op jit(solution)/shard_map/ppermute | solution.py:188
  29.6 1.2 %copy-start = (bf16[64,6656]{1,0:T(8,128)(2,1)S(1)}, bf16[64,6656]{1,0:T(8,128)(2,1)}, u32[]{:S(2)}) copy-start(bf16[64,6656]{1,0:T(8,128)(2,1)} %refs_0_.3) | copy-start | bytes 2555908
  39.5 16.9 %collective-permute-start.11 = (bf16[64,3328]{1,0:T(8,128)(2,1)S(1)}, bf16[64,3328]{1,0:T(8,128)(2,1)S(1)}, u32[]{:S(2)}, u32[]{:S(2)}) collective-permute-start(bf16[64,3328]{1,0:T(8,128)(2,1)S(1)} %after.6.refs_4_), channel_id=1, source_target_pairs={{4,0},{8,12},{5,1},{9,13},{6,2},{10,14},{7,3},{11,15},{20,16},{24,... | collective-permute-start | bytes 1277960 | tf_op jit(solution)/shard_map/ppermute | solution.py:188
  46.3 29.7 %copy-start.1 = (f32[2048]{0:T(1024)S(1)}, f32[2048]{0:T(1024)}, u32[]{:S(2)}) copy-start(f32[2048]{0:T(1024)} %param.8) | copy-start | bytes 24580
  46.3 29.7 %copy-start.2 = (f32[64]{0:T(128)S(1)}, f32[64]{0:T(128)}, u32[]{:S(2)}) copy-start(f32[64]{0:T(128)} %param.6) | copy-start | bytes 772
  47.3 16.2 %collective-permute-start.9 = (bf16[64,3328]{1,0:T(8,128)(2,1)S(1)}, bf16[64,3328]{1,0:T(8,128)(2,1)S(1)}, u32[]{:S(2)}, u32[]{:S(2)}) collective-permute-start(bf16[64,3328]{1,0:T(8,128)(2,1)S(1)} %after.5.refs_4_), channel_id=1, source_target_pairs={{4,0},{8,12},{5,1},{9,13},{6,2},{10,14},{7,3},{11,15},{20,16},{24,... | collective-permute-start | bytes 1277960 | tf_op jit(solution)/shard_map/ppermute | solution.py:188
  48.6 1.6 %collective-permute-start.4 = (bf16[64,2048]{1,0:T(8,128)(2,1)S(1)}, bf16[64,2048]{1,0:T(8,128)(2,1)S(1)}, u32[]{:S(2)}, u32[]{:S(2)}) collective-permute-start(bf16[64,2048]{1,0:T(8,128)(2,1)S(1)} %get-tuple-element.11), channel_id=1, source_target_pairs={{0,1},{1,0},{2,3},{3,2},{4,5},{5,4},{6,7},{7,6},{8,9},{9,8},{10,11... | collective-permute-start | bytes 786440 | tf_op jit(solution)/shard_map/ppermute | solution.py:287
  65.8 1.6 %collective-permute-start.12 = (bf16[64,2048]{1,0:T(8,128)(2,1)S(1)}, bf16[64,2048]{1,0:T(8,128)(2,1)S(1)}, u32[]{:S(2)}, u32[]{:S(2)}) collective-permute-start(bf16[64,2048]{1,0:T(8,128)(2,1)S(1)} %get-tuple-element.14), channel_id=1, source_target_pairs={{0,1},{1,0},{2,3},{3,2},{4,5},{5,4},{6,7},{7,6},{8,9},{9,8},{10,11... | collective-permute-start | bytes 786440 | tf_op jit(solution)/shard_map/ppermute | solution.py:301
  67.6 8.4 %collective-permute-start.13 = (bf16[64,2048]{1,0:T(8,128)(2,1)S(1)}, bf16[64,2048]{1,0:T(8,128)(2,1)S(1)}, u32[]{:S(2)}, u32[]{:S(2)}) collective-permute-start(bf16[64,2048]{1,0:T(8,128)(2,1)S(1)} %get-tuple-element.15), channel_id=1, source_target_pairs={{0,2},{1,3},{2,0},{3,1},{4,6},{5,7},{6,4},{7,5},{8,10},{9,11},{10,... | collective-permute-start | bytes 786440 | tf_op jit(solution)/shard_map/ppermute | solution.py:301
